TPU v7x, 128 devices: a whole 4x4x4 slice. The times are simulated.
128 devices in a mesh: ctx: 32 (over y, z_lo, x), tp: 4 (over z_hi, core).
Axes of the slice: x: 4, y: 4, z: 4 (z_hi: 2, z_lo: 2; z = z_hi * 2 + z_lo), core: 2. Of those that a mesh axis runs over, the one named last changes fastest.
Arguments:
- balance_list: int32 [8192], replicated, may hold values from 0 to 8191, as said below
- doc_ids: int32 [8192], replicated, may hold values from 0 to 15, never falling along the last dimension, each value on 1 to 2048 neighbouring positions
- raw_queries: bfloat16 [8192, 4096], P('ctx', 'tp'), may hold values from -120 to 120
- raw_keys: bfloat16 [8192, 512], P('ctx', 'tp'), may hold values from -6 to 6
- values: bfloat16 [8192, 512], P('ctx', 'tp'), may hold values from -6 to 6
- out_weight: bfloat16 [4096, 8192], P(None, 'tp'), may hold values from -0.375 to 0.375
Outputs:
- layer_out: bfloat16 [8192, 8192], P('ctx', 'tp')
Inputs may be any that keep to these rules, and one draw needn't show every extreme that they name: `balance_list`: A permutation of the 8192 positions. Entries j * 256 to (j + 1) * 256 - 1 list the tokens that device j of ctx holds after rebalancing. Token t first lies on device t // 256. The tokens one device gives to one owner come in whole groups of 4; at most 4 such groups (16 tokens) go to one owner, and in every draw each device gives exactly 4 groups to some owner. `doc_ids`: document numbers never fall along the sequence.
All inputs are finite; a program needn't handle non-finite values.
Results may differ from a plain program's by a relative error of at most 0.012.
Values may be sent and summed in bfloat16 or wider, within the bound.
A program may use at most 64 MiB of HBM per device.

v0:
```python
import math

import jax
import jax.numpy as jnp
from jax import lax
from jax.sharding import PartitionSpec as P

HD = 128


ROPE_BASE = 500000.0


def rotate(matrix, positions):
    row_count = matrix.shape[0]
    col_count = matrix.shape[1]
    head_count = col_count // HD
    half_dim = HD // 2
    vectors = matrix.astype(jnp.float32).reshape(row_count, head_count, HD)
    frequency = ROPE_BASE ** (-(jnp.arange(half_dim, dtype=jnp.float32) * 2.0 / HD))
    angles = positions.astype(jnp.float32)[:, None] * frequency[None, :]
    cosine = jnp.cos(angles)[:, None, :]
    sine = jnp.sin(angles)[:, None, :]
    first_half = vectors[..., :half_dim]
    second_half = vectors[..., half_dim:]
    rotated = jnp.concatenate(
        [first_half * cosine - second_half * sine, second_half * cosine + first_half * sine],
        axis=-1,
    )
    return rotated.reshape(row_count, col_count).astype(jnp.bfloat16)


def on_device(balance_list, doc_ids, raw_queries, raw_keys, values, out_weight):
    ctx_count = lax.axis_size("ctx")
    my_index = lax.axis_index("ctx")
    local_rows = raw_queries.shape[0]
    seq_len = balance_list.shape[0]
    capacity = 4 * (local_rows // (2 * ctx_count))
    scale = 1.0 / math.sqrt(HD)
    home_pos = my_index * local_rows + jnp.arange(local_rows, dtype=jnp.int32)
    q_rot = rotate(raw_queries, home_pos)
    k_rot = rotate(raw_keys, home_pos)
    source = balance_list // local_rows
    source_grid = source.reshape(ctx_count, local_rows)
    device_ids = jnp.arange(ctx_count, dtype=jnp.int32)
    matches = (source_grid[:, :, None] == device_ids[None, None, :]).astype(jnp.int32)
    slot_flat = (jnp.sum(jnp.cumsum(matches, axis=1) * matches, axis=2) - 1).reshape(-1)
    owner_of = jnp.arange(seq_len, dtype=jnp.int32) // local_rows
    target = jnp.where(source == my_index, owner_of * capacity + slot_flat, ctx_count * capacity)
    send_table = jnp.full((ctx_count * capacity,), local_rows, jnp.int32)
    send_table = send_table.at[target].set(balance_list - my_index * local_rows, mode="drop")
    owned = lax.dynamic_slice_in_dim(balance_list, my_index * local_rows, local_rows)
    owned_slot = lax.dynamic_slice_in_dim(slot_flat, my_index * local_rows, local_rows)
    receive_at = owned // local_rows * capacity + owned_slot

    def pack_rows(matrix):
        padded = jnp.concatenate([matrix, jnp.zeros((1, matrix.shape[1]), matrix.dtype)], axis=0)
        return padded[send_table]

    arrived = (
        lax.all_to_all(pack_rows(q_rot), "ctx", split_axis=0, concat_axis=0, tiled=True),
        lax.all_to_all(pack_rows(k_rot), "ctx", split_axis=0, concat_axis=0, tiled=True),
        lax.all_to_all(pack_rows(values), "ctx", split_axis=0, concat_axis=0, tiled=True),
    )
    q_owned = arrived[0][receive_at]
    key_send = arrived[1][receive_at]
    value_send = arrived[2][receive_at]

    def key_info(start, count):
        key_pos = lax.dynamic_slice_in_dim(balance_list, start, count)
        return (key_pos, jnp.take(doc_ids, key_pos))

    query_doc = jnp.take(doc_ids, owned)
    groups = key_send.shape[1] // HD
    per_group = q_owned.shape[1] // HD // groups
    grouped = q_owned.reshape(local_rows, groups, per_group, HD)

    def attend(state, key_rows, value_rows, key_pos, key_doc):
        allowed = (key_doc[None, :] == query_doc[:, None]) & (key_pos[None, :] <= owned[:, None])

        def update(inner):
            running_max, running_sum, accumulated = inner
            key_grouped = key_rows.reshape(-1, groups, HD)
            value_grouped = value_rows.reshape(-1, groups, HD)
            scores = (
                jnp.einsum(
                    "tghd,kgd->ghtk", grouped, key_grouped, preferred_element_type=jnp.float32
                )
                * scale
            )
            scores = jnp.where(allowed[None, None], scores, -1e30)
            new_max = jnp.maximum(running_max, jnp.max(scores, axis=-1))
            weights = jnp.where(allowed[None, None], jnp.exp(scores - new_max[..., None]), 0.0)
            rescale = jnp.exp(running_max - new_max)
            new_sum = running_sum * rescale + jnp.sum(weights, axis=-1)
            contrib = jnp.einsum(
                "ghtk,kgd->tghd",
                weights.astype(jnp.bfloat16),
                value_grouped,
                preferred_element_type=jnp.float32,
            )
            new_acc = accumulated * jnp.transpose(rescale, (2, 0, 1))[..., None] + contrib
            return (new_max, new_sum, new_acc)

        def keep(inner):
            return inner

        return lax.cond(jnp.any(allowed), update, keep, state)

    initial = (
        jnp.full((groups, per_group, local_rows), -1e30, jnp.float32),
        jnp.zeros((groups, per_group, local_rows), jnp.float32),
        jnp.zeros((local_rows, groups, per_group, HD), jnp.float32),
    )
    state = initial
    key_piece = lax.all_gather(key_send, "ctx", axis=0, tiled=True)
    value_piece = lax.all_gather(value_send, "ctx", axis=0, tiled=True)
    piece_rows = key_piece.shape[0]
    block_rows = min(piece_rows, 1024)
    whole_blocks = piece_rows // block_rows

    def one_block(block, inner):
        offset = block * block_rows
        key_rows = lax.dynamic_slice_in_dim(key_piece, offset, block_rows)
        value_rows = lax.dynamic_slice_in_dim(value_piece, offset, block_rows)
        key_pos, key_doc = key_info(offset, block_rows)
        return attend(inner, key_rows, value_rows, key_pos, key_doc)

    state = lax.fori_loop(0, whole_blocks, one_block, state)
    running_max, running_sum, accumulated = state
    attention = accumulated / jnp.transpose(running_sum, (2, 0, 1))[..., None]
    attention = attention.reshape(local_rows, groups * per_group * HD).astype(jnp.bfloat16)
    summed = jnp.dot(
        lax.all_gather(attention, "tp", axis=1, tiled=True),
        out_weight,
        preferred_element_type=jnp.float32,
    )
    return summed.astype(jnp.bfloat16)


def solution(mesh):
    in_specs = (P(), P(), P("ctx", "tp"), P("ctx", "tp"), P("ctx", "tp"), P(None, "tp"))
    out_specs = P("ctx", "tp")
    return jax.shard_map(
        on_device, mesh=mesh, in_specs=in_specs, out_specs=out_specs, check_vma=False
    )
```

profile of v0, /device:TPU:1, one launch (start us, length us, event | category | flops | bytes accessed | tf_op | source)
XLA Modules:
  0.0 569.5 jit_solution(15185220578550912120)
XLA Ops:
  7.6 18.4 %reduce-window.6 = s32[32,32,2,128]{3,1,2,0:T(8,128)S(1)} reduce-window(s32[32,32,2,128]{3,1,2,0:T(8,128)S(1)} %fusion.28, s32[]{:T(128)} %constant.154.clone.1), window={size=1x1x1x128 pad=0_0x0_0x0_0x127_0}, to_apply=%region_0.1 | reduce-window | flops 33292288 | bytes 2097156 | tf_op jit(solution)/shard_map/reduce-window
  28.2 30.4 %scatter_custom_fusion = s32[512]{0:T(512)S(1)} fusion(s32[8192]{0:T(1024)S(1)} %get-tuple-element.342, s32[8192]{0:T(1024)S(1)} %get-tuple-element.341, s32[]{:T(128)} %constant.159.clone.1), kind=kCustom, calls=%fused_computation.99 | custom fusion | bytes 2052 | tf_op jit(solution)/shard_map/scatter | solution.py:51
  61.4 9.2 %all-to-all-start.2 = ((bf16[32,16,128]{2,1,0:T(8,128)(2,1)}), bf16[32,16,128]{2,1,0:T(8,128)(2,1)S(1)}, u32[]{:S(2)}, u32[]{:S(2)}) async-start(bf16[32,16,128]{2,1,0:T(8,128)(2,1)} %bitcast.23), calls=%async_computation.2 | async-start | bytes 262144 | tf_op jit(solution)/shard_map/all_to_all | solution.py:63
  71.5 6.8 %all-to-all-done.2 = bf16[32,16,128]{2,1,0:T(8,128)(2,1)S(1)} async-done(((bf16[32,16,128]{2,1,0:T(8,128)(2,1)}), bf16[32,16,128]{2,1,0:T(8,128)(2,1)S(1)}, u32[]{:S(2)}, u32[]{:S(2)}) %all-to-all-start.2) | async-done | bytes 131104 | tf_op jit(solution)/shard_map/all_to_all | solution.py:63
  81.8 11.1 %all_to_all.36 = bf16[32,16,128]{2,1,0:T(8,128)(2,1)S(1)} all-to-all(bf16[32,16,128]{2,1,0:T(8,128)(2,1)S(1)} %bitcast.117), channel_id=1, replica_groups=mesh['ctx'=32,'tp'=4] {'ctx'}, dimensions={0} | all-to-all | bytes 262144 | tf_op jit(solution)/shard_map/all_to_all | solution.py:62
  104.9 13.1 %all-to-all-done.1 = bf16[32,16,1024]{2,1,0:T(8,128)(2,1)S(1)} async-done(((bf16[32,16,1024]{2,1,0:T(8,128)(2,1)}), bf16[32,16,1024]{2,1,0:T(8,128)(2,1)S(1)}, u32[]{:S(2)}, u32[]{:S(2)}) %all-to-all-start.1) | async-done | bytes 1048608 | tf_op jit(solution)/shard_map/all_to_all | solution.py:61
  119.4 94.4 %all-gather.10.cloned.1.call-done = bf16[8192,128]{1,0:T(8,128)(2,1)} async-done(((bf16[256,128]{1,0:T(8,128)(2,1)}), bf16[8192,128]{1,0:T(8,128)(2,1)}) %all-gather.10.cloned.1.call-update) | async-done | bytes 2097168 | tf_op jit(solution)/shard_map/all_gather | solution.py:117
  217.9 151.7 %all-gather.8.cloned.1.call-done = bf16[8192,128]{1,0:T(8,128)(2,1)} async-done(((bf16[256,128]{1,0:T(8,128)(2,1)}), bf16[8192,128]{1,0:T(8,128)(2,1)}) %all-gather.8.cloned.1.call-update) | async-done | bytes 2097168 | tf_op jit(solution)/shard_map/all_gather | solution.py:116
  369.7 132.7 %while.17 = (s32[]{:T(128)}, f32[1,8,256]{2,1,0:T(8,128)S(1)}, f32[1,8,256]{2,1,0:T(8,128)S(1)}, f32[256,1,8,128]{0,3,2,1:T(8,128)S(1)}, s32[8192]{0:T(1024)}, /...) while((s32[]{:T(128)}, f32[1,8,256]{2,1,0:T(8,128)S(1)}, ...), condition=%wide.region_10.11_spmd, body=%wide.region_4.10_spmd.sunk | while | flops 1102595072 | bytes 29539644 | solution.py:129
  378.4 7.8 %conditional.2 = ((f32[1,8,256]{2,1,0:T(8,128)S(1)}, f32[1,8,256]{2,1,0:T(8,128)S(1)}, f32[256,1,8,128]{0,3,2,1:T(8,128)S(1)})) conditional(s32[]{:T(128)} %convert_element_type.64, (f32[1,8,256]{2,1,0:T(8,128)S(1)}, f32[1,8,256]{2,1,0:T(8,128)S(1)}, f32[256,1,8,128]{0,3,2,1:T(8,128)S(1)}) %tuple.57, (pred[256,1024]{0,1:T(8,128)(4,1)S(1)}, ...), branch_computations={%region_6.6_spmd, %region_7.9_spmd} | conditional | flops 1101535232 | bytes 29230112 | solution.py:108
  387.0 6.1 %gather_fusion = s32[1024]{0:T(1024)S(1)} fusion(s32[8192]{0:T(1024)S(1)} %get-tuple-element.467, s32[1024]{0:T(1024)S(1)} %get-tuple-element.420), kind=kCustom, calls=%fused_computation.clone.1 | custom fusion | bytes 12288 | tf_op jit(solution)/shard_map/while/body/eval_jaxpr/jit(_take)/gather | solution.py:71
  395.0 7.8 %conditional.2 = ((f32[1,8,256]{2,1,0:T(8,128)S(1)}, f32[1,8,256]{2,1,0:T(8,128)S(1)}, f32[256,1,8,128]{0,3,2,1:T(8,128)S(1)})) conditional(s32[]{:T(128)} %convert_element_type.64, (f32[1,8,256]{2,1,0:T(8,128)S(1)}, f32[1,8,256]{2,1,0:T(8,128)S(1)}, f32[256,1,8,128]{0,3,2,1:T(8,128)S(1)}) %tuple.57, (pred[256,1024]{0,1:T(8,128)(4,1)S(1)}, ...), branch_computations={%region_6.6_spmd, %region_7.9_spmd} | conditional | flops 1101535232 | bytes 29230112 | solution.py:108
  403.6 6.1 %gather_fusion = s32[1024]{0:T(1024)S(1)} fusion(s32[8192]{0:T(1024)S(1)} %get-tuple-element.467, s32[1024]{0:T(1024)S(1)} %get-tuple-element.420), kind=kCustom, calls=%fused_computation.clone.1 | custom fusion | bytes 12288 | tf_op jit(solution)/shard_map/while/body/eval_jaxpr/jit(_take)/gather | solution.py:71
  411.6 7.8 %conditional.2 = ((f32[1,8,256]{2,1,0:T(8,128)S(1)}, f32[1,8,256]{2,1,0:T(8,128)S(1)}, f32[256,1,8,128]{0,3,2,1:T(8,128)S(1)})) conditional(s32[]{:T(128)} %convert_element_type.64, (f32[1,8,256]{2,1,0:T(8,128)S(1)}, f32[1,8,256]{2,1,0:T(8,128)S(1)}, f32[256,1,8,128]{0,3,2,1:T(8,128)S(1)}) %tuple.57, (pred[256,1024]{0,1:T(8,128)(4,1)S(1)}, ...), branch_computations={%region_6.6_spmd, %region_7.9_spmd} | conditional | flops 1101535232 | bytes 29230112 | solution.py:108
  420.1 6.1 %gather_fusion = s32[1024]{0:T(1024)S(1)} fusion(s32[8192]{0:T(1024)S(1)} %get-tuple-element.467, s32[1024]{0:T(1024)S(1)} %get-tuple-element.420), kind=kCustom, calls=%fused_computation.clone.1 | custom fusion | bytes 12288 | tf_op jit(solution)/shard_map/while/body/eval_jaxpr/jit(_take)/gather | solution.py:71
  428.2 7.8 %conditional.2 = ((f32[1,8,256]{2,1,0:T(8,128)S(1)}, f32[1,8,256]{2,1,0:T(8,128)S(1)}, f32[256,1,8,128]{0,3,2,1:T(8,128)S(1)})) conditional(s32[]{:T(128)} %convert_element_type.64, (f32[1,8,256]{2,1,0:T(8,128)S(1)}, f32[1,8,256]{2,1,0:T(8,128)S(1)}, f32[256,1,8,128]{0,3,2,1:T(8,128)S(1)}) %tuple.57, (pred[256,1024]{0,1:T(8,128)(4,1)S(1)}, ...), branch_computations={%region_6.6_spmd, %region_7.9_spmd} | conditional | flops 1101535232 | bytes 29230112 | solution.py:108
  436.7 6.1 %gather_fusion = s32[1024]{0:T(1024)S(1)} fusion(s32[8192]{0:T(1024)S(1)} %get-tuple-element.467, s32[1024]{0:T(1024)S(1)} %get-tuple-element.420), kind=kCustom, calls=%fused_computation.clone.1 | custom fusion | bytes 12288 | tf_op jit(solution)/shard_map/while/body/eval_jaxpr/jit(_take)/gather | solution.py:71
  444.8 7.8 %conditional.2 = ((f32[1,8,256]{2,1,0:T(8,128)S(1)}, f32[1,8,256]{2,1,0:T(8,128)S(1)}, f32[256,1,8,128]{0,3,2,1:T(8,128)S(1)})) conditional(s32[]{:T(128)} %convert_element_type.64, (f32[1,8,256]{2,1,0:T(8,128)S(1)}, f32[1,8,256]{2,1,0:T(8,128)S(1)}, f32[256,1,8,128]{0,3,2,1:T(8,128)S(1)}) %tuple.57, (pred[256,1024]{0,1:T(8,128)(4,1)S(1)}, ...), branch_computations={%region_6.6_spmd, %region_7.9_spmd} | conditional | flops 1101535232 | bytes 29230112 | solution.py:108
  453.3 6.1 %gather_fusion = s32[1024]{0:T(1024)S(1)} fusion(s32[8192]{0:T(1024)S(1)} %get-tuple-element.467, s32[1024]{0:T(1024)S(1)} %get-tuple-element.420), kind=kCustom, calls=%fused_computation.clone.1 | custom fusion | bytes 12288 | tf_op jit(solution)/shard_map/while/body/eval_jaxpr/jit(_take)/gather | solution.py:71
  461.3 7.8 %conditional.2 = ((f32[1,8,256]{2,1,0:T(8,128)S(1)}, f32[1,8,256]{2,1,0:T(8,128)S(1)}, f32[256,1,8,128]{0,3,2,1:T(8,128)S(1)})) conditional(s32[]{:T(128)} %convert_element_type.64, (f32[1,8,256]{2,1,0:T(8,128)S(1)}, f32[1,8,256]{2,1,0:T(8,128)S(1)}, f32[256,1,8,128]{0,3,2,1:T(8,128)S(1)}) %tuple.57, (pred[256,1024]{0,1:T(8,128)(4,1)S(1)}, ...), branch_computations={%region_6.6_spmd, %region_7.9_spmd} | conditional | flops 1101535232 | bytes 29230112 | solution.py:108
  477.9 7.8 %conditional.2 = ((f32[1,8,256]{2,1,0:T(8,128)S(1)}, f32[1,8,256]{2,1,0:T(8,128)S(1)}, f32[256,1,8,128]{0,3,2,1:T(8,128)S(1)})) conditional(s32[]{:T(128)} %convert_element_type.64, (f32[1,8,256]{2,1,0:T(8,128)S(1)}, f32[1,8,256]{2,1,0:T(8,128)S(1)}, f32[256,1,8,128]{0,3,2,1:T(8,128)S(1)}) %tuple.57, (pred[256,1024]{0,1:T(8,128)(4,1)S(1)}, ...), branch_computations={%region_6.6_spmd, %region_7.9_spmd} | conditional | flops 1101535232 | bytes 29230112 | solution.py:108
  494.5 7.8 %conditional.2 = ((f32[1,8,256]{2,1,0:T(8,128)S(1)}, f32[1,8,256]{2,1,0:T(8,128)S(1)}, f32[256,1,8,128]{0,3,2,1:T(8,128)S(1)})) conditional(s32[]{:T(128)} %convert_element_type.64, (f32[1,8,256]{2,1,0:T(8,128)S(1)}, f32[1,8,256]{2,1,0:T(8,128)S(1)}, f32[256,1,8,128]{0,3,2,1:T(8,128)S(1)}) %tuple.57, (pred[256,1024]{0,1:T(8,128)(4,1)S(1)}, ...), branch_computations={%region_6.6_spmd, %region_7.9_spmd} | conditional | flops 1101535232 | bytes 29230112 | solution.py:108
  503.3 47.8 %all-gather.6.cloned.1.call-done = bf16[256,4096]{0,1:T(8,128)(2,1)} async-done(((bf16[256,1024]{0,1:T(8,128)(2,1)}), bf16[256,4096]{0,1:T(8,128)(2,1)}) %all-gather.6.cloned.1.call-update) | async-done | bytes 2097168 | tf_op jit(solution)/shard_map/all_gather | solution.py:134
  551.1 11.9 %convolution_convert_fusion = bf16[256,2048]{1,0:T(8,128)(2,1)} fusion(bf16[256,4096]{0,1:T(8,128)(2,1)} %all-gather.6.cloned.1.call-done, bf16[4096,2048]{1,0:T(8,128)(2,1)} %param.15), kind=kOutput, calls=%fused_computation.38 | convolution fusion | flops 4295491584 | bytes 19922944 | tf_op jit(solution)/shard_map/dot_general | solution.py:133
  (137 shorter events, 125.1 us)
Async XLA Ops:
  6.5 73.3 %copy-start.2 = (bf16[256,128]{1,0:T(8,128)(2,1)S(1)}, bf16[256,128]{1,0:T(8,128)(2,1)}, u32[]{:S(2)}) copy-start(bf16[256,128]{1,0:T(8,128)(2,1)} %param.13) | copy-start | bytes 196612
  6.5 87.8 %copy-start.1 = (bf16[256,1024]{1,0:T(8,128)(2,1)S(1)}, bf16[256,1024]{1,0:T(8,128)(2,1)}, u32[]{:S(2)}) copy-start(bf16[256,1024]{1,0:T(8,128)(2,1)} %param.12) | copy-start | bytes 1572868
  61.4 16.8 %all-to-all-start.2 = ((bf16[32,16,128]{2,1,0:T(8,128)(2,1)}), bf16[32,16,128]{2,1,0:T(8,128)(2,1)S(1)}, u32[]{:S(2)}, u32[]{:S(2)}) async-start(bf16[32,16,128]{2,1,0:T(8,128)(2,1)} %bitcast.23), calls=%async_computation.2 | async-start | bytes 262144 | tf_op jit(solution)/shard_map/all_to_all | solution.py:63
  70.6 143.1 %all-gather.10.cloned.1.call-start = ((), (), s32[]{:S(2)}) async-start(), calls=%async_computation.5 | async-start | bytes 2162688 | tf_op jit(solution)/shard_map/all_gather | solution.py:117
  79.7 289.8 %all-gather.8.cloned.1.call-start = ((), (), s32[]{:S(2)}) async-start(), calls=%async_computation.4 | async-start | bytes 2162688 | tf_op jit(solution)/shard_map/all_gather | solution.py:116
  95.7 7.4 %copy-start = (s32[8192]{0:T(1024)S(1)}, s32[8192]{0:T(1024)}, u32[]{:S(2)}) copy-start(s32[8192]{0:T(1024)} %param.11) | copy-start | bytes 98308
  98.9 19.1 %all-to-all-start.1 = ((bf16[32,16,1024]{2,1,0:T(8,128)(2,1)}), bf16[32,16,1024]{2,1,0:T(8,128)(2,1)S(1)}, u32[]{:S(2)}, u32[]{:S(2)}) async-start(bf16[32,16,1024]{2,1,0:T(8,128)(2,1)} %bitcast.21), calls=%async_computation.1 | async-start | bytes 2097152 | tf_op jit(solution)/shard_map/all_to_all | solution.py:61
  102.9 448.2 %all-gather.6.cloned.1.call-start = ((), (), s32[]{:S(2)}) async-start(), calls=%async_computation.3 | async-start | bytes 2621440 | tf_op jit(solution)/shard_map/all_gather | solution.py:134
Sparse Core Ops, SparseCore 0:
  79.9 133.8 all-gather.9
  215.4 154.0 all-gather.7
  503.4 47.6 all-gather.5
where the time goes:
time: 571 us; the launch traced here: 569 us
  waiting for transfers between devices  314 us (55%)
  local copies, waits for them, and re-layouts  98.1 us (17%)
  matrix products  57.9 us (10%)
  other arithmetic  56.4 us (10%)
  starting transfers between devices  13.5 us (2%)
  between operations  13.4 us (2%)
  blocking collectives  11.1 us (2%)
    all_gather x1, waiting for transfers between devices, on_device(): key_piece = lax.all_gather(key_send, 'ctx', axis=0, tiled=True)  152 us
    all_gather x1, waiting for transfers between devices, on_device(): value_piece = lax.all_gather(value_send, 'ctx', axis=0, tiled=True)  94.4 us
    gather x8, local copies, waits for them, and re-layouts, key_info(): return (key_pos, jnp.take(doc_ids, key_pos))  49.2 us
    all_gather x1, waiting for transfers between devices, on_device(): lax.all_gather(attention, 'tp', axis=1, tiled=True)  47.8 us
    scatter x1, local copies, waits for them, and re-layouts, on_device(): send_table.at[target].set(balance_list - my_index * local_rows, mode='drop')  30.4 us
    dot_general x8, matrix products, update(): jnp.einsum('ghtk,kgd->tghd', weights.astype(jnp.bfloat16), value_grouped,...  27.3 us
    another operation x4, other arithmetic  19.3 us
    dot_general x8, matrix products, update(): jnp.einsum('tghd,kgd->ghtk', grouped, key_grouped, preferred_element_type...  18.7 us
  transfers between devices with their start and end apart: 5, of which 5 were waited for; matrix products, arithmetic and copies ran while one was open for 3% of the time, Pallas kernels for 0%

commit v1 on v0

v1 whole, which is shorter than its diff:
```python
import functools
import math

import jax
import jax.numpy as jnp
import numpy as np
from jax import lax
from jax.experimental import pallas as pl
from jax.experimental.pallas import tpu as pltpu
from jax.sharding import PartitionSpec as P

MESH = pl.DeviceIdType.MESH
HD = 128
NCTX = 32
ROWS = 256
HEADS = 8
BACK = 8
SLOTS = 16
CHUNKS = 4
PER_CHUNK = HEADS // CHUNKS
WIDTH = HEADS * HD // CHUNKS
OUT = 2048
FAR = 1048576.0
ROPE_BASE = 500000.0
F32 = jnp.float32
BF16 = jnp.bfloat16


def rope_tables():
    freq = ROPE_BASE ** (-(np.arange(HD // 2, dtype=np.float64) * 2.0 / HD))
    freq = np.concatenate([freq, freq])[None, :]
    inner = np.arange(ROWS, dtype=np.float64)[:, None] * freq
    outer = (np.arange(NCTX, dtype=np.float64) * ROWS)[:, None] * freq
    inner = np.stack([np.cos(inner), np.sin(inner)]).astype(np.float32)
    outer = np.stack([np.cos(outer), np.sin(outer)]).astype(np.float32)
    return inner, outer


def iota(shape, dim):
    return lax.broadcasted_iota(jnp.int32, shape, dim)


def kernel(
    bl, docs, q_in, k_in, v_in, inner, outer, w_hbm, out,
    qx, kv, feat, scores, tops, code, local, pack_m, unpack_m, packed, landed, merged, gath, w, acc,
    kv_send, kv_recv, a_send, a_recv, n_send, n_recv, z_send, z_recv, c_send, c_recv, f_send, f_recv, w_sem,
):
    me = lax.axis_index("ctx")
    tp = lax.axis_index("tp")
    hi, core = tp // 2, tp % 2
    mate = hi * 2 + 1 - core
    across = (1 - hi) * 2 + core
    across_mate = (1 - hi) * 2 + 1 - core
    twin = me + 4 - 8 * ((me // 4) % 2)

    w_copy = pltpu.make_async_copy(w_hbm, w, w_sem)
    w_copy.start()

    barrier = pltpu.get_barrier_semaphore()

    def greet(d, carry):
        pl.semaphore_signal(barrier, inc=1, device_id=((me + d) % NCTX, tp), device_id_type=MESH)
        return carry

    lax.fori_loop(1, NCTX, greet, 0)
    pl.semaphore_signal(barrier, inc=1, device_id=(me, mate), device_id_type=MESH)
    pl.semaphore_signal(barrier, inc=1, device_id=(twin, across), device_id_type=MESH)

    cos_o = outer[0, pl.ds(me, 1), :]
    sin_o = outer[1, pl.ds(me, 1), :]
    cos = cos_o * inner[0] - sin_o * inner[1]
    sin = sin_o * inner[0] + cos_o * inner[1]
    lane = iota((ROWS, HD), 1)
    sin = jnp.where(lane < HD // 2, -sin, sin)

    def rotate(x):
        x = x.astype(F32)
        return (x * cos + pltpu.roll(x, HD // 2, 1) * sin).astype(BF16)

    kv[0, 0:HD, :] = jnp.transpose(rotate(k_in[...]).astype(F32)).astype(BF16)
    kv[0, HD : 2 * HD, 0:HD] = v_in[0:HD, :]
    kv[0, HD : 2 * HD, HD : 2 * HD] = v_in[HD : 2 * HD, :]

    pl.semaphore_wait(barrier, NCTX + 1)

    def key_copy(source, d, to):
        return pltpu.make_async_remote_copy(
            src_ref=kv.at[source],
            dst_ref=kv.at[d],
            send_sem=kv_send.at[d - 1],
            recv_sem=kv_recv.at[d - 1],
            device_id=((me + to + NCTX) % NCTX, tp),
            device_id_type=MESH,
        )

    for d in (1, 7, 3, 5, 4, 8):
        key_copy(0, d, d).start()

    def doc_row(block):
        row = jnp.concatenate([docs[pl.ds(2 * block, 1), :], docs[pl.ds(2 * block + 1, 1), :]], axis=1)
        return jnp.broadcast_to(row, (HD, ROWS))

    far = jnp.where(jnp.transpose(doc_row(me).astype(F32)) == lane.astype(F32), 0.0, -FAR).astype(BF16)
    for h in range(HEADS):
        c, at = h // PER_CHUNK, h % PER_CHUNK * ROWS
        qx[c, at : at + ROWS, 0:HD] = rotate(q_in[:, h * HD : (h + 1) * HD])
        qx[c, at : at + ROWS, HD : 2 * HD] = far

    doc_iota = iota((HD, ROWS), 0)

    def features(d, carry):
        feat[d] = jnp.where(doc_row((me - d + NCTX) % NCTX) == doc_iota, 1.0, 0.0).astype(BF16)
        return carry

    lax.fori_loop(0, BACK + 1, features, 0)

    square_r, square_c = iota((ROWS, ROWS), 0), iota((ROWS, ROWS), 1)
    lists = jnp.concatenate(
        [bl[pl.ds(0, NCTX, stride=2), :], bl[pl.ds(1, NCTX, stride=2), :]], axis=1
    )
    mine = (lists >> 8) == me
    before = jnp.where(square_r < square_c, 1.0, 0.0).astype(BF16)
    rank = jnp.dot(jnp.where(mine, 1.0, 0.0).astype(BF16), before, preferred_element_type=F32)
    code[...] = jnp.where(mine, rank, -1.0)
    local[...] = ((lists & 255) + 1).astype(F32)
    slot_iota = iota((SLOTS, ROWS), 0).astype(F32)
    lane_next = (iota((SLOTS, ROWS), 1) + 1).astype(F32)

    def pack_rows(o, carry):
        hit = code[pl.ds(o, 1), :] == slot_iota
        token = jnp.sum(jnp.where(hit, local[pl.ds(o, 1), :], 0.0), axis=1, keepdims=True)
        at = pl.multiple_of(o * SLOTS, SLOTS)
        pack_m[pl.ds(at, SLOTS), :] = jnp.where(token == lane_next, 1.0, 0.0).astype(BF16)
        return carry

    lax.fori_loop(0, NCTX, pack_rows, 0)

    own = jnp.concatenate([bl[pl.ds(2 * twin, 1), :], bl[pl.ds(2 * twin + 1, 1), :]], axis=1)
    source_row = (own >> 8).astype(F32)
    source_col = jnp.sum(jnp.where(square_r == square_c, source_row, 0.0), axis=1, keepdims=True)
    earlier = (source_row == source_col) & (square_c < square_r)
    slot_col = jnp.sum(jnp.where(earlier, 1.0, 0.0), axis=1, keepdims=True)
    place = source_col * SLOTS + slot_col
    wide = iota((ROWS, NCTX * SLOTS), 1).astype(F32)
    unpack_m[...] = jnp.where(wide == place, 1.0, 0.0).astype(BF16)

    factor = math.log2(math.e) / math.sqrt(HD)
    chunk_rows = PER_CHUNK * ROWS

    def score(d):
        def one(c, carry):
            keys = jnp.concatenate([kv[d, 0:HD, :], feat[d]], axis=0)
            part = jnp.dot(qx[c], keys, preferred_element_type=F32) * factor
            if d == 0:
                part = jnp.where(
                    iota((chunk_rows, ROWS), 1) <= (iota((chunk_rows, ROWS), 0) & (ROWS - 1)), part, -2.0 * FAR
                )
            scores[c, d] = part
            top = jnp.maximum(part[:, 0:HD], part[:, HD:])
            tops[c] = top if d == 0 else jnp.maximum(tops[c], top)
            return carry

        lax.fori_loop(0, CHUNKS, one, 0)

    score(0)
    key_copy(0, 1, 1).wait_recv()
    key_copy(1, 2, 1).start()
    key_copy(0, 7, 7).wait_recv()
    key_copy(7, 6, -1).start()
    score(1)
    score(7)
    for d in (3, 5, 4, 8, 2, 6):
        key_copy(0, d, d).wait_recv()
        score(d)

    def attend(c, carry):
        ones = jnp.ones((ROWS, HD), BF16)
        vals = []
        for d in range(BACK + 1):
            block = jnp.concatenate([kv[d, HD : 2 * HD, 0:HD], kv[d, HD : 2 * HD, HD : 2 * HD]], axis=0)
            vals.append(jnp.concatenate([block, ones], axis=1))
        vals = jnp.concatenate(vals, axis=0)
        part = []
        for h in range(PER_CHUNK):
            rows = slice(h * ROWS, (h + 1) * ROWS)
            top = jnp.max(tops[c, rows, :], axis=1, keepdims=True)
            weights = [jnp.exp2(scores[c, d, rows, :] - top).astype(BF16) for d in range(BACK + 1)]
            mixed = jnp.dot(jnp.concatenate(weights, axis=1), vals, preferred_element_type=F32)
            part.append((mixed[:, 0:HD] / mixed[:, HD : 2 * HD]).astype(BF16))
        part = jnp.concatenate(part, axis=1)
        rows = jnp.dot(pack_m[...], part, preferred_element_type=F32).astype(BF16)
        packed[c] = rows.reshape(NCTX, SLOTS, WIDTH)
        landed[c, me] = packed[c, twin]

        def send(d, inner_carry):
            to = (me + d) % NCTX
            pltpu.make_async_remote_copy(
                src_ref=packed.at[c, to + 4 - 8 * ((to // 4) % 2)],
                dst_ref=landed.at[c, me],
                send_sem=a_send.at[c],
                recv_sem=a_recv.at[c],
                device_id=(to, tp),
                device_id_type=MESH,
            ).start()
            return inner_carry

        return lax.fori_loop(1, NCTX, send, carry)

    lax.fori_loop(0, CHUNKS, attend, 0)

    def hand(c, to, sems):
        return pltpu.make_async_remote_copy(
            src_ref=merged.at[c],
            dst_ref=gath.at[c, tp],
            send_sem=sems[0].at[c],
            recv_sem=sems[1].at[c],
            device_id=(twin, to),
            device_id_type=MESH,
        )

    near, far_off, mate_near, mate_far = (n_send, n_recv), (z_send, z_recv), (c_send, c_recv), (f_send, f_recv)

    def share(c, slot, sems):
        return pltpu.make_async_remote_copy(
            src_ref=gath.at[c, slot],
            dst_ref=gath.at[c, slot],
            send_sem=sems[0].at[c],
            recv_sem=sems[1].at[c],
            device_id=(me, mate),
            device_id_type=MESH,
        )

    def unpack(c):
        rest = packed.at[c, pl.ds(0, NCTX - 1)]
        pltpu.make_async_copy(rest, rest, a_recv.at[c]).wait()
        rows = jnp.dot(unpack_m[...], landed[c].reshape(NCTX * SLOTS, WIDTH), preferred_element_type=F32)
        merged[c] = rows.astype(BF16)
        hand(c, tp, near).start()
        hand(c, across, far_off).start()

    def forward(c):
        hand(c, tp, near).wait_recv()
        share(c, tp, mate_near).start()
        hand(c, across, far_off).wait_recv()
        share(c, across, mate_far).start()

    def project(c):
        share(c, mate, mate_near).wait_recv()
        share(c, across_mate, mate_far).wait_recv()

        def columns(n, carry):
            cols = pl.ds(pl.multiple_of(n * 512, 512), 512)
            total = jnp.zeros((ROWS, 512), F32)
            for t in range(4):
                first = t * HEADS * HD + c * WIDTH
                total += jnp.dot(gath[c, t], w[first : first + WIDTH, cols], preferred_element_type=F32)
            if c > 0:
                total += acc[:, cols]
            if c < CHUNKS - 1:
                acc[:, cols] = total
            else:
                out[:, cols] = total.astype(BF16)
            return carry

        lax.fori_loop(0, OUT // 512, columns, 0)

    unpack(0)
    unpack(1)
    forward(0)
    unpack(2)
    forward(1)
    w_copy.wait()
    project(0)
    unpack(3)
    forward(2)
    project(1)
    forward(3)
    project(2)
    project(3)

    for d in range(1, BACK + 1):
        key_copy(0, d, d).wait_send()
    for c in range(CHUNKS):
        rest = packed.at[c, pl.ds(0, NCTX - 1)]
        pltpu.make_async_copy(rest, rest, a_send.at[c]).wait()
        hand(c, tp, near).wait_send()
        hand(c, across, far_off).wait_send()
        share(c, tp, mate_near).wait_send()
        share(c, across, mate_far).wait_send()


def on_device(balance_list, doc_ids, raw_queries, raw_keys, values, out_weight):
    inner, outer = rope_tables()
    vmem = pl.BlockSpec(memory_space=pltpu.VMEM)
    dma = pltpu.SemaphoreType.DMA
    return pl.pallas_call(
        kernel,
        out_shape=jax.ShapeDtypeStruct((ROWS, OUT), BF16),
        in_specs=[vmem] * 7 + [pl.BlockSpec(memory_space=pl.ANY)],
        out_specs=vmem,
        scratch_shapes=[
            pltpu.VMEM((CHUNKS, PER_CHUNK * ROWS, 2 * HD), BF16),
            pltpu.VMEM((BACK + 1, ROWS, 2 * HD), BF16),
            pltpu.VMEM((BACK + 1, HD, ROWS), BF16),
            pltpu.VMEM((CHUNKS, BACK + 1, PER_CHUNK * ROWS, ROWS), F32),
            pltpu.VMEM((CHUNKS, PER_CHUNK * ROWS, HD), F32),
            pltpu.VMEM((NCTX, ROWS), F32),
            pltpu.VMEM((NCTX, ROWS), F32),
            pltpu.VMEM((NCTX * SLOTS, ROWS), BF16),
            pltpu.VMEM((ROWS, NCTX * SLOTS), BF16),
            pltpu.VMEM((CHUNKS, NCTX, SLOTS, WIDTH), BF16),
            pltpu.VMEM((CHUNKS, NCTX, SLOTS, WIDTH), BF16),
            pltpu.VMEM((CHUNKS, ROWS, WIDTH), BF16),
            pltpu.VMEM((CHUNKS, 4, ROWS, WIDTH), BF16),
            pltpu.VMEM((4096, OUT), BF16),
            pltpu.VMEM((ROWS, OUT), F32),
            dma((BACK,)), dma((BACK,)),
            dma((CHUNKS,)), dma((CHUNKS,)),
            dma((CHUNKS,)), dma((CHUNKS,)),
            dma((CHUNKS,)), dma((CHUNKS,)),
            dma((CHUNKS,)), dma((CHUNKS,)),
            dma((CHUNKS,)), dma((CHUNKS,)),
            dma,
        ],
        compiler_params=pltpu.CompilerParams(
            collective_id=0, has_side_effects=True, vmem_limit_bytes=56 * 1024 * 1024
        ),
        cost_estimate=pl.CostEstimate(
            flops=7_000_000_000, bytes_accessed=19_000_000, transcendentals=4_700_000
        ),
    )(
        balance_list.reshape(64, 128), doc_ids.reshape(64, 128), raw_queries, raw_keys, values,
        jnp.asarray(inner), jnp.asarray(outer), out_weight,
    )


def solution(mesh):
    in_specs = (P(), P(), P("ctx", "tp"), P("ctx", "tp"), P("ctx", "tp"), P(None, "tp"))
    out_specs = P("ctx", "tp")
    return jax.shard_map(
        on_device, mesh=mesh, in_specs=in_specs, out_specs=out_specs, check_vma=False
    )
```

time: 571 us -> 66.9 us (0.12)
  the two profiles are of different devices: /device:TPU:1 before, /device:TPU:4 now
where the time goes in v1:
time: 66.9 us; the launch traced here: 66.8 us
  Pallas kernels  64.5 us (96%)
  local copies, waits for them, and re-layouts  2.3 us (3%)
    pallas_call x1, Pallas kernels, on_device(): pl.pallas_call(kernel, out_shape=jax.ShapeDtypeStruct((ROWS, OUT), BF16),...  64.5 us
    unnamed x1, local copies, waits for them, and re-layouts  2.3 us

profile of v1, /device:TPU:4, one launch (start us, length us, event | category | flops | bytes accessed | tf_op | source)
XLA Modules:
  0.0 66.8 jit_solution(3902393605047658024)
XLA Ops:
  0.0 64.5 %shard_map.82 = bf16[256,2048]{1,0:T(8,128)(2,1)} custom-call(s32[64,128]{1,0:T(8,128)} %bitcast.2, s32[64,128]{1,0:T(8,128)} %bitcast.3, bf16[256,1024]{1,0:T(8,128)(2,1)} %q_in.1, bf16[256,128]{1,0:T(8,128)(2,1)} %k_in.1, bf16[256,128]{1,0:T(8,128)(2,1)} %v_in.1, f32[2,256,128]{2,1,0:T(8,128)} %constant.4.clone.inner, f32[2,32,128]{2,1,0:T(8,128)} %constant.5.clone.outer, ...), custom_call_target="tpu_custom_call" | custom-call | flops 7000000000 | bytes 19000000 | tf_op jit(solution)/shard_map/pallas_call | solution.py:296
  64.5 2.3 %copy.10 = bf16[256,2048]{1,0:T(8,128)(2,1)} copy(bf16[256,2048]{1,0:T(8,128)(2,1)} %shard_map.82) | data formatting | bytes 2097152

commit v2 on v1

--- a/solution.py
+++ b/solution.py
@@ -17,6 +17,7 @@
 BACK = 8
 SLOTS = 16
 CHUNKS = 4
+LAG = 3
 PER_CHUNK = HEADS // CHUNKS
 WIDTH = HEADS * HD // CHUNKS
 OUT = 2048
@@ -41,9 +42,10 @@
 
 
 def kernel(
-    bl, docs, q_in, k_in, v_in, inner, outer, w_hbm, out,
+    bl_h, docs_h, q_h, k_h, v_h, inner_h, outer_h, w_hbm, out,
+    bl, docs, q_in, k_in, v_in, inner, outer,
     qx, kv, feat, scores, tops, code, local, pack_m, unpack_m, packed, landed, merged, gath, w, acc,
-    kv_send, kv_recv, a_send, a_recv, n_send, n_recv, z_send, z_recv, c_send, c_recv, f_send, f_recv, w_sem,
+    kv_send, kv_recv, a_send, a_recv, n_send, n_recv, z_send, z_recv, c_send, c_recv, f_send, f_recv, w_sem, in_sem,
 ):
     me = lax.axis_index("ctx")
     tp = lax.axis_index("tp")
@@ -54,18 +56,29 @@
     twin = me + 4 - 8 * ((me // 4) % 2)
 
     w_copy = pltpu.make_async_copy(w_hbm, w, w_sem)
-    w_copy.start()
+    pairs = (
+        (k_h, k_in), (inner_h, inner), (outer_h, outer), (v_h, v_in), (q_h, q_in), (docs_h, docs), (bl_h, bl)
+    )
+    loads = [pltpu.make_async_copy(a, b, in_sem.at[n]) for n, (a, b) in enumerate(pairs)]
+    for load in loads:
+        load.start()
 
     barrier = pltpu.get_barrier_semaphore()
 
-    def greet(d, carry):
-        pl.semaphore_signal(barrier, inc=1, device_id=((me + d) % NCTX, tp), device_id_type=MESH)
-        return carry
-
-    lax.fori_loop(1, NCTX, greet, 0)
+    def others(body):
+        lax.fori_loop(me + 1, NCTX, body, 0)
+        lax.fori_loop(0, me, body, 0)
+
+    def greet(to, carry):
+        pl.semaphore_signal(barrier, inc=1, device_id=(to, tp), device_id_type=MESH)
+        return carry
+
+    others(greet)
     pl.semaphore_signal(barrier, inc=1, device_id=(me, mate), device_id_type=MESH)
     pl.semaphore_signal(barrier, inc=1, device_id=(twin, across), device_id_type=MESH)
 
+    for load in loads[:4]:
+        load.wait()
     cos_o = outer[0, pl.ds(me, 1), :]
     sin_o = outer[1, pl.ds(me, 1), :]
     cos = cos_o * inner[0] - sin_o * inner[1]
@@ -89,22 +102,47 @@
             dst_ref=kv.at[d],
             send_sem=kv_send.at[d - 1],
             recv_sem=kv_recv.at[d - 1],
-            device_id=((me + to + NCTX) % NCTX, tp),
+            device_id=(to, tp),
             device_id_type=MESH,
         )
 
-    for d in (1, 7, 3, 5, 4, 8):
-        key_copy(0, d, d).start()
+    slab, place_in = me // BACK * BACK, me % BACK
+    key_copy(0, BACK, (me + BACK) % NCTX).start()
+
+    def send_own(d, carry):
+        @pl.when(place_in + d < BACK)
+        def _():
+            key_copy(0, d, me + d).start()
+
+        return carry
+
+    def send_previous(d, carry):
+        @pl.when(place_in + d >= BACK)
+        def _():
+            key_copy(BACK, d, slab + (place_in + d) % BACK).start()
+
+        return carry
+
+    lax.fori_loop(1, BACK, send_own, 0)
+    w_copy.start()
+    for load in loads[4:]:
+        load.wait()
 
     def doc_row(block):
         row = jnp.concatenate([docs[pl.ds(2 * block, 1), :], docs[pl.ds(2 * block + 1, 1), :]], axis=1)
         return jnp.broadcast_to(row, (HD, ROWS))
 
     far = jnp.where(jnp.transpose(doc_row(me).astype(F32)) == lane.astype(F32), 0.0, -FAR).astype(BF16)
-    for h in range(HEADS):
-        c, at = h // PER_CHUNK, h % PER_CHUNK * ROWS
-        qx[c, at : at + ROWS, 0:HD] = rotate(q_in[:, h * HD : (h + 1) * HD])
-        qx[c, at : at + ROWS, HD : 2 * HD] = far
+
+    def queries(h, carry):
+        rows = pl.ds(pl.multiple_of(h * ROWS, ROWS), ROWS)
+        qx[rows, 0:HD] = rotate(q_in[:, pl.ds(pl.multiple_of(h * HD, HD), HD)])
+        qx[rows, HD : 2 * HD] = far
+        return carry
+
+    lax.fori_loop(0, HEADS, queries, 0)
+    key_copy(0, BACK, me).wait_recv()
+    lax.fori_loop(1, BACK, send_previous, 0)
 
     doc_iota = iota((HD, ROWS), 0)
 
@@ -129,11 +167,11 @@
     def pack_rows(o, carry):
         hit = code[pl.ds(o, 1), :] == slot_iota
         token = jnp.sum(jnp.where(hit, local[pl.ds(o, 1), :], 0.0), axis=1, keepdims=True)
-        at = pl.multiple_of(o * SLOTS, SLOTS)
+        at = pl.multiple_of((o + 4 - 8 * ((o // 4) % 2)) * SLOTS, SLOTS)
         pack_m[pl.ds(at, SLOTS), :] = jnp.where(token == lane_next, 1.0, 0.0).astype(BF16)
         return carry
 
-    lax.fori_loop(0, NCTX, pack_rows, 0)
+    lax.fori_loop(0, NCTX, pack_rows, 0, unroll=8)
 
     own = jnp.concatenate([bl[pl.ds(2 * twin, 1), :], bl[pl.ds(2 * twin + 1, 1), :]], axis=1)
     source_row = (own >> 8).astype(F32)
@@ -147,33 +185,36 @@
     factor = math.log2(math.e) / math.sqrt(HD)
     chunk_rows = PER_CHUNK * ROWS
 
-    def score(d):
-        def one(c, carry):
-            keys = jnp.concatenate([kv[d, 0:HD, :], feat[d]], axis=0)
-            part = jnp.dot(qx[c], keys, preferred_element_type=F32) * factor
-            if d == 0:
-                part = jnp.where(
-                    iota((chunk_rows, ROWS), 1) <= (iota((chunk_rows, ROWS), 0) & (ROWS - 1)), part, -2.0 * FAR
-                )
+    def score_own(c, carry):
+        keys = jnp.concatenate([kv[0, 0:HD, :], feat[0]], axis=0)
+        rows = pl.ds(pl.multiple_of(c * chunk_rows, chunk_rows), chunk_rows)
+        part = jnp.dot(qx[rows, :], keys, preferred_element_type=F32) * factor
+        allowed = iota((chunk_rows, ROWS), 1) <= (iota((chunk_rows, ROWS), 0) & (ROWS - 1))
+        part = jnp.where(allowed, part, -2.0 * FAR)
+        scores[c, 0] = part
+        tops[c] = jnp.maximum(part[:, 0:HD], part[:, HD:])
+        return carry
+
+    lax.fori_loop(0, CHUNKS, score_own, 0)
+
+    def score(i, carry):
+        d = (i + BACK - 1) % BACK + 1
+
+        @pl.when(i > 0)
+        def _():
+            key_copy(0, d, me).wait_recv()
+
+        keys = jnp.concatenate([kv[d, 0:HD, :], feat[d]], axis=0)
+        for c in range(CHUNKS):
+            rows = slice(c * chunk_rows, (c + 1) * chunk_rows)
+            part = jnp.dot(qx[rows, :], keys, preferred_element_type=F32) * factor
             scores[c, d] = part
-            top = jnp.maximum(part[:, 0:HD], part[:, HD:])
-            tops[c] = top if d == 0 else jnp.maximum(tops[c], top)
-            return carry
-
-        lax.fori_loop(0, CHUNKS, one, 0)
-
-    score(0)
-    key_copy(0, 1, 1).wait_recv()
-    key_copy(1, 2, 1).start()
-    key_copy(0, 7, 7).wait_recv()
-    key_copy(7, 6, -1).start()
-    score(1)
-    score(7)
-    for d in (3, 5, 4, 8, 2, 6):
-        key_copy(0, d, d).wait_recv()
-        score(d)
-
-    def attend(c, carry):
+            tops[c] = jnp.maximum(tops[c], jnp.maximum(part[:, 0:HD], part[:, HD:]))
+        return carry
+
+    lax.fori_loop(0, BACK, score, 0)
+
+    def attend(c):
         ones = jnp.ones((ROWS, HD), BF16)
         vals = []
         for d in range(BACK + 1):
@@ -190,12 +231,11 @@
         part = jnp.concatenate(part, axis=1)
         rows = jnp.dot(pack_m[...], part, preferred_element_type=F32).astype(BF16)
         packed[c] = rows.reshape(NCTX, SLOTS, WIDTH)
-        landed[c, me] = packed[c, twin]
-
-        def send(d, inner_carry):
-            to = (me + d) % NCTX
+        landed[c, me] = packed[c, me]
+
+        def send(to, inner_carry):
             pltpu.make_async_remote_copy(
-                src_ref=packed.at[c, to + 4 - 8 * ((to // 4) % 2)],
+                src_ref=packed.at[c, to],
                 dst_ref=landed.at[c, me],
                 send_sem=a_send.at[c],
                 recv_sem=a_recv.at[c],
@@ -204,9 +244,7 @@
             ).start()
             return inner_carry
 
-        return lax.fori_loop(1, NCTX, send, carry)
-
-    lax.fori_loop(0, CHUNKS, attend, 0)
+        others(send)
 
     def hand(c, to, sems):
         return pltpu.make_async_remote_copy(
@@ -244,42 +282,54 @@
         hand(c, across, far_off).wait_recv()
         share(c, across, mate_far).start()
 
-    def project(c):
+    def project(c, final):
         share(c, mate, mate_near).wait_recv()
         share(c, across_mate, mate_far).wait_recv()
+        rows = jnp.concatenate([gath[c, t] for t in range(4)], axis=1)
 
         def columns(n, carry):
             cols = pl.ds(pl.multiple_of(n * 512, 512), 512)
-            total = jnp.zeros((ROWS, 512), F32)
-            for t in range(4):
-                first = t * HEADS * HD + c * WIDTH
-                total += jnp.dot(gath[c, t], w[first : first + WIDTH, cols], preferred_element_type=F32)
-            if c > 0:
-                total += acc[:, cols]
-            if c < CHUNKS - 1:
+            part = [
+                w[pl.ds(pl.multiple_of(t * HEADS * HD + c * WIDTH, WIDTH), WIDTH), cols] for t in range(4)
+            ]
+            total = jnp.dot(rows, jnp.concatenate(part, axis=0), preferred_element_type=F32) + acc[:, cols]
+            if final:
+                out[:, cols] = total.astype(BF16)
+            else:
                 acc[:, cols] = total
-            else:
-                out[:, cols] = total.astype(BF16)
             return carry
 
         lax.fori_loop(0, OUT // 512, columns, 0)
 
-    unpack(0)
-    unpack(1)
-    forward(0)
-    unpack(2)
-    forward(1)
-    w_copy.wait()
-    project(0)
-    unpack(3)
-    forward(2)
-    project(1)
-    forward(3)
-    project(2)
-    project(3)
+    def step(s, carry):
+        @pl.when((s >= LAG) & (s < CHUNKS + LAG))
+        def _():
+            unpack(s - LAG)
+
+        @pl.when(s < CHUNKS)
+        def _():
+            attend(s)
+
+        @pl.when((s >= LAG + 1) & (s < CHUNKS + LAG + 1))
+        def _():
+            forward(s - LAG - 1)
+
+        @pl.when(s == LAG + 1)
+        def _():
+            w_copy.wait()
+
+        @pl.when(s >= LAG + 2)
+        def _():
+            project(s - LAG - 2, False)
+
+        return carry
+
+    acc[...] = jnp.zeros((ROWS, OUT), F32)
+    lax.fori_loop(0, CHUNKS + LAG + 1, step, 0)
+    project(CHUNKS - 1, True)
 
     for d in range(1, BACK + 1):
-        key_copy(0, d, d).wait_send()
+        key_copy(0, d, me).wait_send()
     for c in range(CHUNKS):
         rest = packed.at[c, pl.ds(0, NCTX - 1)]
         pltpu.make_async_copy(rest, rest, a_send.at[c]).wait()
@@ -296,10 +346,17 @@
     return pl.pallas_call(
         kernel,
         out_shape=jax.ShapeDtypeStruct((ROWS, OUT), BF16),
-        in_specs=[vmem] * 7 + [pl.BlockSpec(memory_space=pl.ANY)],
+        in_specs=[pl.BlockSpec(memory_space=pl.ANY)] * 8,
         out_specs=vmem,
         scratch_shapes=[
-            pltpu.VMEM((CHUNKS, PER_CHUNK * ROWS, 2 * HD), BF16),
+            pltpu.VMEM((64, 128), jnp.int32),
+            pltpu.VMEM((64, 128), jnp.int32),
+            pltpu.VMEM((ROWS, HEADS * HD), BF16),
+            pltpu.VMEM((ROWS, HD), BF16),
+            pltpu.VMEM((ROWS, HD), BF16),
+            pltpu.VMEM((2, ROWS, HD), F32),
+            pltpu.VMEM((2, NCTX, HD), F32),
+            pltpu.VMEM((HEADS * ROWS, 2 * HD), BF16),
             pltpu.VMEM((BACK + 1, ROWS, 2 * HD), BF16),
             pltpu.VMEM((BACK + 1, HD, ROWS), BF16),
             pltpu.VMEM((CHUNKS, BACK + 1, PER_CHUNK * ROWS, ROWS), F32),
@@ -321,9 +378,10 @@
             dma((CHUNKS,)), dma((CHUNKS,)),
             dma((CHUNKS,)), dma((CHUNKS,)),
             dma,
+            dma((7,)),
         ],
         compiler_params=pltpu.CompilerParams(
-            collective_id=0, has_side_effects=True, vmem_limit_bytes=56 * 1024 * 1024
+            collective_id=0, has_side_effects=True, vmem_limit_bytes=60 * 1024 * 1024
         ),
         cost_estimate=pl.CostEstimate(
             flops=7_000_000_000, bytes_accessed=19_000_000, transcendentals=4_700_000

time: 66.9 us -> 61.4 us (0.918)
  the two profiles are of different devices: /device:TPU:4 before, /device:TPU:1 now
where the time goes in v2:
time: 61.4 us; the launch traced here: 61.2 us
  Pallas kernels  58.9 us (96%)
  local copies, waits for them, and re-layouts  2.3 us (4%)
    pallas_call x1, Pallas kernels, on_device(): pl.pallas_call(kernel, out_shape=jax.ShapeDtypeStruct((ROWS, OUT), BF16),...  58.9 us
    unnamed x1, local copies, waits for them, and re-layouts  2.3 us

profile of v2, /device:TPU:1, one launch (start us, length us, event | category | flops | bytes accessed | tf_op | source)
XLA Modules:
  0.0 61.2 jit_solution(12159719619427039594)
XLA Ops:
  0.0 58.9 %shard_map.82 = bf16[256,2048]{1,0:T(8,128)(2,1)} custom-call(s32[64,128]{1,0:T(8,128)} %bitcast.2, s32[64,128]{1,0:T(8,128)} %bitcast.3, bf16[256,1024]{1,0:T(8,128)(2,1)} %q_h.1, bf16[256,128]{1,0:T(8,128)(2,1)} %k_h.1, bf16[256,128]{1,0:T(8,128)(2,1)} %v_h.1, f32[2,256,128]{2,1,0:T(8,128)} %constant.4.clone.inner_h, f32[2,32,128]{2,1,0:T(8,128)} %constant.5.clone.outer_h, ...), custom_call_target="tpu_custom_call" | custom-call | flops 7000000000 | bytes 19000000 | tf_op jit(solution)/shard_map/pallas_call | solution.py:346
  58.9 2.3 %copy.10 = bf16[256,2048]{1,0:T(8,128)(2,1)} copy(bf16[256,2048]{1,0:T(8,128)(2,1)} %shard_map.82) | data formatting | bytes 2097152

commit v3 on v2

--- a/solution.py
+++ b/solution.py
@@ -12,6 +12,7 @@
 MESH = pl.DeviceIdType.MESH
 HD = 128
 NCTX = 32
+PLANE = 16
 ROWS = 256
 HEADS = 8
 BACK = 8
@@ -44,8 +45,8 @@
 def kernel(
     bl_h, docs_h, q_h, k_h, v_h, inner_h, outer_h, w_hbm, out,
     bl, docs, q_in, k_in, v_in, inner, outer,
-    qx, kv, feat, scores, tops, code, local, pack_m, unpack_m, packed, landed, merged, gath, w, acc,
-    kv_send, kv_recv, a_send, a_recv, n_send, n_recv, z_send, z_recv, c_send, c_recv, f_send, f_recv, w_sem, in_sem,
+    qx, kv, feat, scores, tops, code, local, pack_m, unpack_m, pair, packed, landed, merged, gath, w, acc,
+    kv_send, kv_recv, p_send, p_recv, a_send, a_recv, h_send, h_recv, c_send, c_recv, w_sem, in_sem,
 ):
     me = lax.axis_index("ctx")
     tp = lax.axis_index("tp")
@@ -53,7 +54,17 @@
     mate = hi * 2 + 1 - core
     across = (1 - hi) * 2 + core
     across_mate = (1 - hi) * 2 + 1 - core
-    twin = me + 4 - 8 * ((me // 4) % 2)
+    lo = (me // 4) % 2
+    twin = me + 4 - 8 * lo
+    mine_xy = me // 8 * 4 + me % 4
+
+    def in_plane(xy):
+        return xy // 4 * 8 + lo * 4 + xy % 4
+
+    def others(body):
+        lax.fori_loop(mine_xy + 1, PLANE, body, 0)
+        lax.fori_loop(0, mine_xy, body, 0)
+
 
     w_copy = pltpu.make_async_copy(w_hbm, w, w_sem)
     pairs = (
@@ -65,17 +76,19 @@
 
     barrier = pltpu.get_barrier_semaphore()
 
-    def others(body):
-        lax.fori_loop(me + 1, NCTX, body, 0)
-        lax.fori_loop(0, me, body, 0)
-
-    def greet(to, carry):
+    def greet(xy, carry):
+        pl.semaphore_signal(barrier, inc=1, device_id=(in_plane(xy), tp), device_id_type=MESH)
+        return carry
+
+    def greet_other_plane(x, carry):
+        to = me // 8 * 8 + (1 - lo) * 4 + x
         pl.semaphore_signal(barrier, inc=1, device_id=(to, tp), device_id_type=MESH)
         return carry
 
+    lax.fori_loop(0, 4, greet_other_plane, 0)
     others(greet)
-    pl.semaphore_signal(barrier, inc=1, device_id=(me, mate), device_id_type=MESH)
-    pl.semaphore_signal(barrier, inc=1, device_id=(twin, across), device_id_type=MESH)
+    for who in ((me, mate), (me, across), (twin, across)):
+        pl.semaphore_signal(barrier, inc=1, device_id=who, device_id_type=MESH)
 
     for load in loads[:4]:
         load.wait()
@@ -94,7 +107,7 @@
     kv[0, HD : 2 * HD, 0:HD] = v_in[0:HD, :]
     kv[0, HD : 2 * HD, HD : 2 * HD] = v_in[HD : 2 * HD, :]
 
-    pl.semaphore_wait(barrier, NCTX + 1)
+    pl.semaphore_wait(barrier, PLANE - 1 + 4 + 3)
 
     def key_copy(source, d, to):
         return pltpu.make_async_remote_copy(
@@ -156,31 +169,41 @@
     lists = jnp.concatenate(
         [bl[pl.ds(0, NCTX, stride=2), :], bl[pl.ds(1, NCTX, stride=2), :]], axis=1
     )
-    mine = (lists >> 8) == me
     before = jnp.where(square_r < square_c, 1.0, 0.0).astype(BF16)
-    rank = jnp.dot(jnp.where(mine, 1.0, 0.0).astype(BF16), before, preferred_element_type=F32)
-    code[...] = jnp.where(mine, rank, -1.0)
     local[...] = ((lists & 255) + 1).astype(F32)
     slot_iota = iota((SLOTS, ROWS), 0).astype(F32)
     lane_next = (iota((SLOTS, ROWS), 1) + 1).astype(F32)
+    for n, source in enumerate((me, twin)):
+        held = (lists >> 8) == source
+        rank = jnp.dot(jnp.where(held, 1.0, 0.0).astype(BF16), before, preferred_element_type=F32)
+        code[n] = jnp.where(held, rank, -1.0)
 
     def pack_rows(o, carry):
-        hit = code[pl.ds(o, 1), :] == slot_iota
-        token = jnp.sum(jnp.where(hit, local[pl.ds(o, 1), :], 0.0), axis=1, keepdims=True)
-        at = pl.multiple_of((o + 4 - 8 * ((o // 4) % 2)) * SLOTS, SLOTS)
-        pack_m[pl.ds(at, SLOTS), :] = jnp.where(token == lane_next, 1.0, 0.0).astype(BF16)
-        return carry
-
-    lax.fori_loop(0, NCTX, pack_rows, 0, unroll=8)
-
-    own = jnp.concatenate([bl[pl.ds(2 * twin, 1), :], bl[pl.ds(2 * twin + 1, 1), :]], axis=1)
-    source_row = (own >> 8).astype(F32)
-    source_col = jnp.sum(jnp.where(square_r == square_c, source_row, 0.0), axis=1, keepdims=True)
-    earlier = (source_row == source_col) & (square_c < square_r)
-    slot_col = jnp.sum(jnp.where(earlier, 1.0, 0.0), axis=1, keepdims=True)
-    place = source_col * SLOTS + slot_col
+        at = pl.multiple_of(((o // 8 * 4 + o % 4) * 2 + (o // 4) % 2) * SLOTS, SLOTS)
+        for n in range(2):
+            hit = code[n, pl.ds(o, 1), :] == slot_iota
+            token = jnp.sum(jnp.where(hit, local[pl.ds(o, 1), :], 0.0), axis=1, keepdims=True)
+            pack_m[n, pl.ds(at, SLOTS), :] = jnp.where(token == lane_next, 1.0, 0.0).astype(BF16)
+        return carry
+
+    lax.fori_loop(0, NCTX, pack_rows, 0, unroll=4)
+
     wide = iota((ROWS, NCTX * SLOTS), 1).astype(F32)
-    unpack_m[...] = jnp.where(wide == place, 1.0, 0.0).astype(BF16)
+
+    def unpack_rows(l, carry):
+        owner = me // 8 * 8 + l * 4 + me % 4
+        own = jnp.concatenate([bl[pl.ds(2 * owner, 1), :], bl[pl.ds(2 * owner + 1, 1), :]], axis=1) >> 8
+        source_row = own.astype(F32)
+        source_col = jnp.sum(jnp.where(square_r == square_c, source_row, 0.0), axis=1, keepdims=True)
+        earlier = (source_row == source_col) & (square_c < square_r)
+        slot_col = jnp.sum(jnp.where(earlier, 1.0, 0.0), axis=1, keepdims=True)
+        spot = ((((own >> 3) * 4 + (own & 3)) * 2 + ((own >> 2) & 1)) * SLOTS).astype(F32)
+        spot_col = jnp.sum(jnp.where(square_r == square_c, spot, 0.0), axis=1, keepdims=True)
+        place = spot_col + slot_col
+        unpack_m[l] = jnp.where(wide == place, 1.0, 0.0).astype(BF16)
+        return carry
+
+    lax.fori_loop(0, 2, unpack_rows, 0)
 
     factor = math.log2(math.e) / math.sqrt(HD)
     chunk_rows = PER_CHUNK * ROWS
@@ -229,62 +252,85 @@
             mixed = jnp.dot(jnp.concatenate(weights, axis=1), vals, preferred_element_type=F32)
             part.append((mixed[:, 0:HD] / mixed[:, HD : 2 * HD]).astype(BF16))
         part = jnp.concatenate(part, axis=1)
-        rows = jnp.dot(pack_m[...], part, preferred_element_type=F32).astype(BF16)
-        packed[c] = rows.reshape(NCTX, SLOTS, WIDTH)
-        landed[c, me] = packed[c, me]
-
-        def send(to, inner_carry):
+        pair[c, lo] = part
+        swap(c).start()
+        spread(c, 0)
+
+    def swap(c):
+        return pltpu.make_async_remote_copy(
+            src_ref=pair.at[c, lo],
+            dst_ref=pair.at[c, lo],
+            send_sem=p_send.at[c],
+            recv_sem=p_recv.at[c],
+            device_id=(twin, tp),
+            device_id_type=MESH,
+        )
+
+    def spread(c, n):
+        source_lo = lo if n == 0 else 1 - lo
+        rows = jnp.dot(pack_m[n], pair[c, source_lo], preferred_element_type=F32).astype(BF16)
+        packed[c, n] = rows.reshape(PLANE, 2, SLOTS, WIDTH)
+        landed[c, :, mine_xy, source_lo] = packed[c, n, mine_xy]
+
+        def send(xy, inner_carry):
             pltpu.make_async_remote_copy(
-                src_ref=packed.at[c, to],
-                dst_ref=landed.at[c, me],
+                src_ref=packed.at[c, n, xy],
+                dst_ref=landed.at[c, :, mine_xy, source_lo],
                 send_sem=a_send.at[c],
                 recv_sem=a_recv.at[c],
-                device_id=(to, tp),
+                device_id=(in_plane(xy), tp),
                 device_id_type=MESH,
             ).start()
             return inner_carry
 
         others(send)
 
-    def hand(c, to, sems):
+    def spread_twin(c):
+        swap(c).wait_recv()
+        spread(c, 1)
+
+    def hand(c):
         return pltpu.make_async_remote_copy(
             src_ref=merged.at[c],
             dst_ref=gath.at[c, tp],
-            send_sem=sems[0].at[c],
-            recv_sem=sems[1].at[c],
-            device_id=(twin, to),
+            send_sem=h_send.at[c],
+            recv_sem=h_recv.at[c],
+            device_id=(twin, across),
             device_id_type=MESH,
         )
 
-    near, far_off, mate_near, mate_far = (n_send, n_recv), (z_send, z_recv), (c_send, c_recv), (f_send, f_recv)
-
-    def share(c, slot, sems):
+    def share(c, slot, n):
         return pltpu.make_async_remote_copy(
             src_ref=gath.at[c, slot],
             dst_ref=gath.at[c, slot],
-            send_sem=sems[0].at[c],
-            recv_sem=sems[1].at[c],
+            send_sem=c_send.at[c, n],
+            recv_sem=c_recv.at[c, n],
             device_id=(me, mate),
             device_id_type=MESH,
         )
 
+    def whole(c):
+        return packed.at[c, :, pl.ds(0, PLANE - 1)]
+
     def unpack(c):
-        rest = packed.at[c, pl.ds(0, NCTX - 1)]
-        pltpu.make_async_copy(rest, rest, a_recv.at[c]).wait()
-        rows = jnp.dot(unpack_m[...], landed[c].reshape(NCTX * SLOTS, WIDTH), preferred_element_type=F32)
-        merged[c] = rows.astype(BF16)
-        hand(c, tp, near).start()
-        hand(c, across, far_off).start()
+        pltpu.make_async_copy(whole(c), whole(c), a_recv.at[c]).wait()
+
+        def merge(l):
+            rows = landed[c, l].reshape(NCTX * SLOTS, WIDTH)
+            return jnp.dot(unpack_m[l], rows, preferred_element_type=F32).astype(BF16)
+
+        merged[c] = merge(1 - lo)
+        hand(c).start()
+        gath[c, tp] = merge(lo)
+        share(c, tp, 0).start()
 
     def forward(c):
-        hand(c, tp, near).wait_recv()
-        share(c, tp, mate_near).start()
-        hand(c, across, far_off).wait_recv()
-        share(c, across, mate_far).start()
+        hand(c).wait_recv()
+        share(c, across, 1).start()
 
     def project(c, final):
-        share(c, mate, mate_near).wait_recv()
-        share(c, across_mate, mate_far).wait_recv()
+        share(c, mate, 0).wait_recv()
+        share(c, across_mate, 1).wait_recv()
         rows = jnp.concatenate([gath[c, t] for t in range(4)], axis=1)
 
         def columns(n, carry):
@@ -310,6 +356,10 @@
         def _():
             attend(s)
 
+        @pl.when((s >= 1) & (s < CHUNKS + 1))
+        def _():
+            spread_twin(s - 1)
+
         @pl.when((s >= LAG + 1) & (s < CHUNKS + LAG + 1))
         def _():
             forward(s - LAG - 1)
@@ -331,12 +381,11 @@
     for d in range(1, BACK + 1):
         key_copy(0, d, me).wait_send()
     for c in range(CHUNKS):
-        rest = packed.at[c, pl.ds(0, NCTX - 1)]
-        pltpu.make_async_copy(rest, rest, a_send.at[c]).wait()
-        hand(c, tp, near).wait_send()
-        hand(c, across, far_off).wait_send()
-        share(c, tp, mate_near).wait_send()
-        share(c, across, mate_far).wait_send()
+        swap(c).wait_send()
+        pltpu.make_async_copy(whole(c), whole(c), a_send.at[c]).wait()
+        hand(c).wait_send()
+        share(c, tp, 0).wait_send()
+        share(c, across, 1).wait_send()
 
 
 def on_device(balance_list, doc_ids, raw_queries, raw_keys, values, out_weight):
@@ -361,12 +410,13 @@
             pltpu.VMEM((BACK + 1, HD, ROWS), BF16),
             pltpu.VMEM((CHUNKS, BACK + 1, PER_CHUNK * ROWS, ROWS), F32),
             pltpu.VMEM((CHUNKS, PER_CHUNK * ROWS, HD), F32),
+            pltpu.VMEM((2, NCTX, ROWS), F32),
             pltpu.VMEM((NCTX, ROWS), F32),
-            pltpu.VMEM((NCTX, ROWS), F32),
-            pltpu.VMEM((NCTX * SLOTS, ROWS), BF16),
-            pltpu.VMEM((ROWS, NCTX * SLOTS), BF16),
-            pltpu.VMEM((CHUNKS, NCTX, SLOTS, WIDTH), BF16),
-            pltpu.VMEM((CHUNKS, NCTX, SLOTS, WIDTH), BF16),
+            pltpu.VMEM((2, NCTX * SLOTS, ROWS), BF16),
+            pltpu.VMEM((2, ROWS, NCTX * SLOTS), BF16),
+            pltpu.VMEM((CHUNKS, 2, ROWS, WIDTH), BF16),
+            pltpu.VMEM((CHUNKS, 2, PLANE, 2, SLOTS, WIDTH), BF16),
+            pltpu.VMEM((CHUNKS, 2, PLANE, 2, SLOTS, WIDTH), BF16),
             pltpu.VMEM((CHUNKS, ROWS, WIDTH), BF16),
             pltpu.VMEM((CHUNKS, 4, ROWS, WIDTH), BF16),
             pltpu.VMEM((4096, OUT), BF16),
@@ -375,8 +425,7 @@
             dma((CHUNKS,)), dma((CHUNKS,)),
             dma((CHUNKS,)), dma((CHUNKS,)),
             dma((CHUNKS,)), dma((CHUNKS,)),
-            dma((CHUNKS,)), dma((CHUNKS,)),
-            dma((CHUNKS,)), dma((CHUNKS,)),
+            dma((CHUNKS, 2)), dma((CHUNKS, 2)),
             dma,
             dma((7,)),
         ],

time: 61.4 us -> 66.1 us (1.077)
  Pallas kernels: 58.9 us -> 63.4 us
    pallas_call x1, Pallas kernels: 58.9 us -> 63.4 us  [on_device(): pl.pallas_call(kernel, out_shape=jax.ShapeDtypeStruct((ROWS, OUT), BF16),...]
where the time goes in v3:
time: 66.1 us; the launch traced here: 65.7 us
  Pallas kernels  63.4 us (96%)
  local copies, waits for them, and re-layouts  2.3 us (3%)
    pallas_call x1, Pallas kernels, on_device(): pl.pallas_call(kernel, out_shape=jax.ShapeDtypeStruct((ROWS, OUT), BF16),...  63.4 us
    unnamed x1, local copies, waits for them, and re-layouts  2.3 us

profile of v3, /device:TPU:1, one launch (start us, length us, event | category | flops | bytes accessed | tf_op | source)
XLA Modules:
  0.0 65.7 jit_solution(13429914501797726077)
XLA Ops:
  0.0 63.4 %shard_map.82 = bf16[256,2048]{1,0:T(8,128)(2,1)} custom-call(s32[64,128]{1,0:T(8,128)} %bitcast.2, s32[64,128]{1,0:T(8,128)} %bitcast.3, bf16[256,1024]{1,0:T(8,128)(2,1)} %q_h.1, bf16[256,128]{1,0:T(8,128)(2,1)} %k_h.1, bf16[256,128]{1,0:T(8,128)(2,1)} %v_h.1, f32[2,256,128]{2,1,0:T(8,128)} %constant.4.clone.inner_h, f32[2,32,128]{2,1,0:T(8,128)} %constant.5.clone.outer_h, ...), custom_call_target="tpu_custom_call" | custom-call | flops 7000000000 | bytes 19000000 | tf_op jit(solution)/shard_map/pallas_call | solution.py:395
  63.4 2.3 %copy.10 = bf16[256,2048]{1,0:T(8,128)(2,1)} copy(bf16[256,2048]{1,0:T(8,128)(2,1)} %shard_map.82) | data formatting | bytes 2097152

commit v4 on v2

--- a/solution.py
+++ b/solution.py
@@ -66,8 +66,7 @@
     barrier = pltpu.get_barrier_semaphore()
 
     def others(body):
-        lax.fori_loop(me + 1, NCTX, body, 0)
-        lax.fori_loop(0, me, body, 0)
+        lax.fori_loop(1, NCTX, lambda d, carry: body(lax.rem(me + d, NCTX), carry), 0, unroll=NCTX - 1)
 
     def greet(to, carry):
         pl.semaphore_signal(barrier, inc=1, device_id=(to, tp), device_id_type=MESH)
@@ -96,32 +95,43 @@
 
     pl.semaphore_wait(barrier, NCTX + 1)
 
-    def key_copy(source, d, to):
+    def key_copy(source, d, to, sem=None):
         return pltpu.make_async_remote_copy(
             src_ref=kv.at[source],
             dst_ref=kv.at[d],
-            send_sem=kv_send.at[d - 1],
+            send_sem=kv_send.at[d - 1 if sem is None else sem],
             recv_sem=kv_recv.at[d - 1],
             device_id=(to, tp),
             device_id_type=MESH,
         )
 
     slab, place_in = me // BACK * BACK, me % BACK
+
+    def direct(d):
+        skip_two = (d == 2) & (place_in != 6)
+        skip_six = (d == 6) & (place_in != 1)
+        return jnp.logical_not(skip_two | skip_six)
+
     key_copy(0, BACK, (me + BACK) % NCTX).start()
 
     def send_own(d, carry):
-        @pl.when(place_in + d < BACK)
+        @pl.when((place_in + d < BACK) & direct(d))
         def _():
             key_copy(0, d, me + d).start()
 
         return carry
 
-    def send_previous(d, carry):
-        @pl.when(place_in + d >= BACK)
+    def send_previous(n, carry):
+        d = BACK - n
+
+        @pl.when((place_in + d >= BACK) & direct(d))
         def _():
             key_copy(BACK, d, slab + (place_in + d) % BACK).start()
 
         return carry
+
+    relay_two = key_copy(1, 2, slab + (place_in + 1) % BACK, BACK)
+    relay_six = key_copy(7, 6, slab + (place_in + 7) % BACK, BACK + 1)
 
     lax.fori_loop(1, BACK, send_own, 0)
     w_copy.start()
@@ -198,11 +208,20 @@
     lax.fori_loop(0, CHUNKS, score_own, 0)
 
     def score(i, carry):
-        d = (i + BACK - 1) % BACK + 1
+        third, seventh, last = (i + 6) // 8 - (i + 5) // 8, (i + 2) // 8, (i + 1) // 8
+        d = (i + BACK - 1) % BACK + 1 + 5 * third - 4 * seventh + 3 * last
 
         @pl.when(i > 0)
         def _():
             key_copy(0, d, me).wait_recv()
+
+        @pl.when((d == 1) & (place_in != 7))
+        def _():
+            relay_two.start()
+
+        @pl.when((d == 7) & (place_in != 0))
+        def _():
+            relay_six.start()
 
         keys = jnp.concatenate([kv[d, 0:HD, :], feat[d]], axis=0)
         for c in range(CHUNKS):
@@ -328,8 +347,16 @@
     lax.fori_loop(0, CHUNKS + LAG + 1, step, 0)
     project(CHUNKS - 1, True)
 
-    for d in range(1, BACK + 1):
-        key_copy(0, d, me).wait_send()
+    def sent(d, carry):
+        @pl.when(direct(d))
+        def _():
+            key_copy(0, d, me).wait_send()
+
+        return carry
+
+    lax.fori_loop(1, BACK + 1, sent, 0)
+    pl.when(place_in != 7)(relay_two.wait_send)
+    pl.when(place_in != 0)(relay_six.wait_send)
     for c in range(CHUNKS):
         rest = packed.at[c, pl.ds(0, NCTX - 1)]
         pltpu.make_async_copy(rest, rest, a_send.at[c]).wait()
@@ -371,7 +398,7 @@
             pltpu.VMEM((CHUNKS, 4, ROWS, WIDTH), BF16),
             pltpu.VMEM((4096, OUT), BF16),
             pltpu.VMEM((ROWS, OUT), F32),
-            dma((BACK,)), dma((BACK,)),
+            dma((BACK + 2,)), dma((BACK,)),
             dma((CHUNKS,)), dma((CHUNKS,)),
             dma((CHUNKS,)), dma((CHUNKS,)),
             dma((CHUNKS,)), dma((CHUNKS,)),

time: 61.4 us -> 61 us (level)
  no operation moved by 1% of the time
where the time goes in v4:
time: 61 us; the launch traced here: 60.8 us
  Pallas kernels  58.5 us (96%)
  local copies, waits for them, and re-layouts  2.3 us (4%)
    pallas_call x1, Pallas kernels, on_device(): pl.pallas_call(kernel, out_shape=jax.ShapeDtypeStruct((ROWS, OUT), BF16),...  58.5 us
    unnamed x1, local copies, waits for them, and re-layouts  2.3 us

profile of v4, /device:TPU:1, one launch (start us, length us, event | category | flops | bytes accessed | tf_op | source)
XLA Modules:
  0.0 60.8 jit_solution(12430461797724700140)
XLA Ops:
  0.0 58.5 %shard_map.82 = bf16[256,2048]{1,0:T(8,128)(2,1)} custom-call(s32[64,128]{1,0:T(8,128)} %bitcast.2, s32[64,128]{1,0:T(8,128)} %bitcast.3, bf16[256,1024]{1,0:T(8,128)(2,1)} %q_h.1, bf16[256,128]{1,0:T(8,128)(2,1)} %k_h.1, bf16[256,128]{1,0:T(8,128)(2,1)} %v_h.1, f32[2,256,128]{2,1,0:T(8,128)} %constant.4.clone.inner_h, f32[2,32,128]{2,1,0:T(8,128)} %constant.5.clone.outer_h, ...), custom_call_target="tpu_custom_call" | custom-call | flops 7000000000 | bytes 19000000 | tf_op jit(solution)/shard_map/pallas_call | solution.py:373
  58.5 2.3 %copy.10 = bf16[256,2048]{1,0:T(8,128)(2,1)} copy(bf16[256,2048]{1,0:T(8,128)(2,1)} %shard_map.82) | data formatting | bytes 2097152

commit v5 on v4

--- a/solution.py
+++ b/solution.py
@@ -27,6 +27,13 @@
 BF16 = jnp.bfloat16
 
 
+def hops(d):
+    return min(d % 4, 4 - d % 4) + min(d // 8, 4 - d // 8) + d // 4 % 2
+
+
+FAR_FIRST = sorted(range(1, NCTX), key=hops, reverse=True)
+
+
 def rope_tables():
     freq = ROPE_BASE ** (-(np.arange(HD // 2, dtype=np.float64) * 2.0 / HD))
     freq = np.concatenate([freq, freq])[None, :]
@@ -66,7 +73,8 @@
     barrier = pltpu.get_barrier_semaphore()
 
     def others(body):
-        lax.fori_loop(1, NCTX, lambda d, carry: body(lax.rem(me + d, NCTX), carry), 0, unroll=NCTX - 1)
+        for d in FAR_FIRST:
+            body(lax.rem(me + d, NCTX), 0)
 
     def greet(to, carry):
         pl.semaphore_signal(barrier, inc=1, device_id=(to, tp), device_id_type=MESH)
@@ -301,24 +309,25 @@
         hand(c, across, far_off).wait_recv()
         share(c, across, mate_far).start()
 
-    def project(c, final):
+    def add_columns(c, slots, target):
+        rows = jnp.concatenate([gath[c, t] for t in slots], axis=1)
+
+        def columns(n, carry):
+            cols = pl.ds(pl.multiple_of(n * 512, 512), 512)
+            part = [w[pl.ds(pl.multiple_of(t * HEADS * HD + c * WIDTH, WIDTH), WIDTH), cols] for t in slots]
+            total = jnp.dot(rows, jnp.concatenate(part, axis=0), preferred_element_type=F32) + acc[:, cols]
+            target[:, cols] = total.astype(target.dtype)
+            return carry
+
+        lax.fori_loop(0, OUT // 512, columns, 0, unroll=2)
+
+    def from_mate(c):
         share(c, mate, mate_near).wait_recv()
         share(c, across_mate, mate_far).wait_recv()
-        rows = jnp.concatenate([gath[c, t] for t in range(4)], axis=1)
-
-        def columns(n, carry):
-            cols = pl.ds(pl.multiple_of(n * 512, 512), 512)
-            part = [
-                w[pl.ds(pl.multiple_of(t * HEADS * HD + c * WIDTH, WIDTH), WIDTH), cols] for t in range(4)
-            ]
-            total = jnp.dot(rows, jnp.concatenate(part, axis=0), preferred_element_type=F32) + acc[:, cols]
-            if final:
-                out[:, cols] = total.astype(BF16)
-            else:
-                acc[:, cols] = total
-            return carry
-
-        lax.fori_loop(0, OUT // 512, columns, 0)
+
+    def project(c):
+        from_mate(c)
+        add_columns(c, range(4), acc)
 
     def step(s, carry):
         @pl.when((s >= LAG) & (s < CHUNKS + LAG))
@@ -339,13 +348,15 @@
 
         @pl.when(s >= LAG + 2)
         def _():
-            project(s - LAG - 2, False)
+            project(s - LAG - 2)
 
         return carry
 
     acc[...] = jnp.zeros((ROWS, OUT), F32)
     lax.fori_loop(0, CHUNKS + LAG + 1, step, 0)
-    project(CHUNKS - 1, True)
+    add_columns(CHUNKS - 1, (tp, across), acc)
+    from_mate(CHUNKS - 1)
+    add_columns(CHUNKS - 1, (mate, across_mate), out)
 
     def sent(d, carry):
         @pl.when(direct(d))
@@ -372,7 +383,7 @@
     dma = pltpu.SemaphoreType.DMA
     return pl.pallas_call(
         kernel,
-        out_shape=jax.ShapeDtypeStruct((ROWS, OUT), BF16),
+        out_shape=pltpu.VMEM((ROWS, OUT), BF16),
         in_specs=[pl.BlockSpec(memory_space=pl.ANY)] * 8,
         out_specs=vmem,
         scratch_shapes=[

time: 61 us -> 57.4 us (0.941)
  Pallas kernels: 58.5 us -> 56.2 us
  local copies, waits for them, and re-layouts: 2.3 us -> 0.97 us
    pallas_call x1, Pallas kernels: 58.5 us -> 56.2 us  [on_device(): pl.pallas_call(kernel, out_shape=pltpu.VMEM((ROWS, OUT), BF16), in_specs=...]
    unnamed x1, local copies, waits for them, and re-layouts: 2.3 us -> 0.97 us
where the time goes in v5:
time: 57.4 us; the launch traced here: 57.2 us
  Pallas kernels  56.2 us (98%)
  local copies, waits for them, and re-layouts  0.97 us (2%)
    pallas_call x1, Pallas kernels, on_device(): pl.pallas_call(kernel, out_shape=pltpu.VMEM((ROWS, OUT), BF16), in_specs=...  56.2 us

profile of v5, /device:TPU:1, one launch (start us, length us, event | category | flops | bytes accessed | tf_op | source)
XLA Modules:
  0.0 57.2 jit_solution(14704008521155691066)
XLA Ops:
  0.0 56.2 %shard_map.82 = bf16[256,2048]{1,0:T(8,128)(2,1)S(1)} custom-call(s32[64,128]{1,0:T(8,128)} %bitcast.2, s32[64,128]{1,0:T(8,128)} %bitcast.3, bf16[256,1024]{1,0:T(8,128)(2,1)} %q_h.1, bf16[256,128]{1,0:T(8,128)(2,1)} %k_h.1, bf16[256,128]{1,0:T(8,128)(2,1)} %v_h.1, f32[2,256,128]{2,1,0:T(8,128)} %constant.4.clone.inner_h, ...), custom_call_target="tpu_custom_call" | custom-call | flops 7000000000 | bytes 19000000 | tf_op jit(solution)/shard_map/pallas_call | solution.py:384
  56.2 1.0 %copy.10 = bf16[256,2048]{1,0:T(8,128)(2,1)} copy(bf16[256,2048]{1,0:T(8,128)(2,1)S(1)} %shard_map.82) | data formatting | bytes 2097152

commit v6 on v5

--- a/solution.py
+++ b/solution.py
@@ -52,7 +52,7 @@
     bl_h, docs_h, q_h, k_h, v_h, inner_h, outer_h, w_hbm, out,
     bl, docs, q_in, k_in, v_in, inner, outer,
     qx, kv, feat, scores, tops, code, local, pack_m, unpack_m, packed, landed, merged, gath, w, acc,
-    kv_send, kv_recv, a_send, a_recv, n_send, n_recv, z_send, z_recv, c_send, c_recv, f_send, f_recv, w_sem, in_sem,
+    kv_send, kv_recv, a_send, a_recv, n_send, n_recv, z_send, z_recv, c_send, c_recv, f_send, f_recv, w_sem, in_sem, ready,
 ):
     me = lax.axis_index("ctx")
     tp = lax.axis_index("tp")
@@ -76,13 +76,21 @@
         for d in FAR_FIRST:
             body(lax.rem(me + d, NCTX), 0)
 
-    def greet(to, carry):
+    slab, place_in = me // BACK * BACK, me % BACK
+    above, below = (me + BACK) % NCTX, (me + NCTX - BACK) % NCTX
+
+    def greet(d, carry):
+        to = slab + (place_in + d) % BACK
         pl.semaphore_signal(barrier, inc=1, device_id=(to, tp), device_id_type=MESH)
         return carry
 
-    others(greet)
-    pl.semaphore_signal(barrier, inc=1, device_id=(me, mate), device_id_type=MESH)
-    pl.semaphore_signal(barrier, inc=1, device_id=(twin, across), device_id_type=MESH)
+    for who in ((above, tp), (below, tp), (me, mate), (twin, across)):
+        pl.semaphore_signal(barrier, inc=1, device_id=who, device_id_type=MESH)
+    lax.fori_loop(1, BACK, greet, 0)
+
+    def tell(n):
+        for to in (above, below):
+            pl.semaphore_signal(ready.at[n], inc=1, device_id=(to, tp), device_id_type=MESH)
 
     for load in loads[:4]:
         load.wait()
@@ -101,45 +109,34 @@
     kv[0, HD : 2 * HD, 0:HD] = v_in[0:HD, :]
     kv[0, HD : 2 * HD, HD : 2 * HD] = v_in[HD : 2 * HD, :]
 
-    pl.semaphore_wait(barrier, NCTX + 1)
-
-    def key_copy(source, d, to, sem=None):
+    pl.semaphore_wait(barrier, BACK - 1 + 4)
+
+    def key_copy(source, d, to):
         return pltpu.make_async_remote_copy(
             src_ref=kv.at[source],
             dst_ref=kv.at[d],
-            send_sem=kv_send.at[d - 1 if sem is None else sem],
+            send_sem=kv_send.at[d - 1],
             recv_sem=kv_recv.at[d - 1],
             device_id=(to, tp),
             device_id_type=MESH,
         )
 
-    slab, place_in = me // BACK * BACK, me % BACK
-
-    def direct(d):
-        skip_two = (d == 2) & (place_in != 6)
-        skip_six = (d == 6) & (place_in != 1)
-        return jnp.logical_not(skip_two | skip_six)
-
-    key_copy(0, BACK, (me + BACK) % NCTX).start()
+    key_copy(0, BACK, above).start()
+    tell(0)
 
     def send_own(d, carry):
-        @pl.when((place_in + d < BACK) & direct(d))
+        @pl.when(place_in + d < BACK)
         def _():
             key_copy(0, d, me + d).start()
 
         return carry
 
-    def send_previous(n, carry):
-        d = BACK - n
-
-        @pl.when((place_in + d >= BACK) & direct(d))
+    def send_previous(d, carry):
+        @pl.when(place_in + d >= BACK)
         def _():
             key_copy(BACK, d, slab + (place_in + d) % BACK).start()
 
         return carry
-
-    relay_two = key_copy(1, 2, slab + (place_in + 1) % BACK, BACK)
-    relay_six = key_copy(7, 6, slab + (place_in + 7) % BACK, BACK + 1)
 
     lax.fori_loop(1, BACK, send_own, 0)
     w_copy.start()
@@ -216,20 +213,11 @@
     lax.fori_loop(0, CHUNKS, score_own, 0)
 
     def score(i, carry):
-        third, seventh, last = (i + 6) // 8 - (i + 5) // 8, (i + 2) // 8, (i + 1) // 8
-        d = (i + BACK - 1) % BACK + 1 + 5 * third - 4 * seventh + 3 * last
+        d = (i + BACK - 1) % BACK + 1
 
         @pl.when(i > 0)
         def _():
             key_copy(0, d, me).wait_recv()
-
-        @pl.when((d == 1) & (place_in != 7))
-        def _():
-            relay_two.start()
-
-        @pl.when((d == 7) & (place_in != 0))
-        def _():
-            relay_six.start()
 
         keys = jnp.concatenate([kv[d, 0:HD, :], feat[d]], axis=0)
         for c in range(CHUNKS):
@@ -239,7 +227,10 @@
             tops[c] = jnp.maximum(tops[c], jnp.maximum(part[:, 0:HD], part[:, HD:]))
         return carry
 
+    pl.semaphore_wait(ready.at[0], 2)
+    tell(1)
     lax.fori_loop(0, BACK, score, 0)
+    pl.semaphore_wait(ready.at[1], 2)
 
     def attend(c):
         ones = jnp.ones((ROWS, HD), BF16)
@@ -358,16 +349,8 @@
     from_mate(CHUNKS - 1)
     add_columns(CHUNKS - 1, (mate, across_mate), out)
 
-    def sent(d, carry):
-        @pl.when(direct(d))
-        def _():
-            key_copy(0, d, me).wait_send()
-
-        return carry
-
-    lax.fori_loop(1, BACK + 1, sent, 0)
-    pl.when(place_in != 7)(relay_two.wait_send)
-    pl.when(place_in != 0)(relay_six.wait_send)
+    for d in range(1, BACK + 1):
+        key_copy(0, d, me).wait_send()
     for c in range(CHUNKS):
         rest = packed.at[c, pl.ds(0, NCTX - 1)]
         pltpu.make_async_copy(rest, rest, a_send.at[c]).wait()
@@ -409,7 +392,7 @@
             pltpu.VMEM((CHUNKS, 4, ROWS, WIDTH), BF16),
             pltpu.VMEM((4096, OUT), BF16),
             pltpu.VMEM((ROWS, OUT), F32),
-            dma((BACK + 2,)), dma((BACK,)),
+            dma((BACK,)), dma((BACK,)),
             dma((CHUNKS,)), dma((CHUNKS,)),
             dma((CHUNKS,)), dma((CHUNKS,)),
             dma((CHUNKS,)), dma((CHUNKS,)),
@@ -417,6 +400,7 @@
             dma((CHUNKS,)), dma((CHUNKS,)),
             dma,
             dma((7,)),
+            pltpu.SemaphoreType.REGULAR((2,)),
         ],
         compiler_params=pltpu.CompilerParams(
             collective_id=0, has_side_effects=True, vmem_limit_bytes=60 * 1024 * 1024

time: 57.4 us -> 57.4 us (level)
  no operation moved by 1% of the time
where the time goes in v6:
time: 57.4 us; the launch traced here: 57.2 us
  Pallas kernels  56.3 us (98%)
  local copies, waits for them, and re-layouts  0.97 us (2%)
    pallas_call x1, Pallas kernels, on_device(): pl.pallas_call(kernel, out_shape=pltpu.VMEM((ROWS, OUT), BF16), in_specs=...  56.3 us

profile of v6, /device:TPU:1, one launch (start us, length us, event | category | flops | bytes accessed | tf_op | source)
XLA Modules:
  0.0 57.2 jit_solution(3187679599679828276)
XLA Ops:
  0.0 56.3 %shard_map.82 = bf16[256,2048]{1,0:T(8,128)(2,1)S(1)} custom-call(s32[64,128]{1,0:T(8,128)} %bitcast.2, s32[64,128]{1,0:T(8,128)} %bitcast.3, bf16[256,1024]{1,0:T(8,128)(2,1)} %q_h.1, bf16[256,128]{1,0:T(8,128)(2,1)} %k_h.1, bf16[256,128]{1,0:T(8,128)(2,1)} %v_h.1, f32[2,256,128]{2,1,0:T(8,128)} %constant.4.clone.inner_h, ...), custom_call_target="tpu_custom_call" | custom-call | flops 7000000000 | bytes 19000000 | tf_op jit(solution)/shard_map/pallas_call | solution.py:367
  56.3 1.0 %copy.10 = bf16[256,2048]{1,0:T(8,128)(2,1)} copy(bf16[256,2048]{1,0:T(8,128)(2,1)S(1)} %shard_map.82) | data formatting | bytes 2097152

commit v7 on v6

--- a/solution.py
+++ b/solution.py
@@ -18,6 +18,7 @@
 SLOTS = 16
 CHUNKS = 4
 LAG = 3
+EARLY = 2
 PER_CHUNK = HEADS // CHUNKS
 WIDTH = HEADS * HD // CHUNKS
 OUT = 2048
@@ -139,7 +140,6 @@
         return carry
 
     lax.fori_loop(1, BACK, send_own, 0)
-    w_copy.start()
     for load in loads[4:]:
         load.wait()
 
@@ -188,14 +188,15 @@
 
     lax.fori_loop(0, NCTX, pack_rows, 0, unroll=8)
 
-    own = jnp.concatenate([bl[pl.ds(2 * twin, 1), :], bl[pl.ds(2 * twin + 1, 1), :]], axis=1)
-    source_row = (own >> 8).astype(F32)
-    source_col = jnp.sum(jnp.where(square_r == square_c, source_row, 0.0), axis=1, keepdims=True)
-    earlier = (source_row == source_col) & (square_c < square_r)
-    slot_col = jnp.sum(jnp.where(earlier, 1.0, 0.0), axis=1, keepdims=True)
-    place = source_col * SLOTS + slot_col
-    wide = iota((ROWS, NCTX * SLOTS), 1).astype(F32)
-    unpack_m[...] = jnp.where(wide == place, 1.0, 0.0).astype(BF16)
+    def merge_table():
+        own = jnp.concatenate([bl[pl.ds(2 * twin, 1), :], bl[pl.ds(2 * twin + 1, 1), :]], axis=1)
+        source_row = (own >> 8).astype(F32)
+        source_col = jnp.sum(jnp.where(square_r == square_c, source_row, 0.0), axis=1, keepdims=True)
+        earlier = (source_row == source_col) & (square_c < square_r)
+        slot_col = jnp.sum(jnp.where(earlier, 1.0, 0.0), axis=1, keepdims=True)
+        place = source_col * SLOTS + slot_col
+        wide = iota((ROWS, NCTX * SLOTS), 1).astype(F32)
+        unpack_m[...] = jnp.where(wide == place, 1.0, 0.0).astype(BF16)
 
     factor = math.log2(math.e) / math.sqrt(HD)
     chunk_rows = PER_CHUNK * ROWS
@@ -210,19 +211,21 @@
         tops[c] = jnp.maximum(part[:, 0:HD], part[:, HD:])
         return carry
 
-    lax.fori_loop(0, CHUNKS, score_own, 0)
+    lax.fori_loop(0, EARLY, score_own, 0)
 
     def score(i, carry):
         d = (i + BACK - 1) % BACK + 1
+        part = pl.ds(pl.multiple_of(i * (4096 // BACK), 4096 // BACK), 4096 // BACK)
+        pltpu.make_async_copy(w_hbm.at[part, :], w.at[part, :], w_sem).start()
 
         @pl.when(i > 0)
         def _():
             key_copy(0, d, me).wait_recv()
 
         keys = jnp.concatenate([kv[d, 0:HD, :], feat[d]], axis=0)
-        for c in range(CHUNKS):
-            rows = slice(c * chunk_rows, (c + 1) * chunk_rows)
-            part = jnp.dot(qx[rows, :], keys, preferred_element_type=F32) * factor
+        every = jnp.dot(qx[0 : EARLY * chunk_rows, :], keys, preferred_element_type=F32) * factor
+        for c in range(EARLY):
+            part = every[c * chunk_rows : (c + 1) * chunk_rows, :]
             scores[c, d] = part
             tops[c] = jnp.maximum(tops[c], jnp.maximum(part[:, 0:HD], part[:, HD:]))
         return carry
@@ -231,6 +234,17 @@
     tell(1)
     lax.fori_loop(0, BACK, score, 0)
     pl.semaphore_wait(ready.at[1], 2)
+
+    def score_late(c):
+        score_own(c, 0)
+        rows = pl.ds(pl.multiple_of(c * chunk_rows, chunk_rows), chunk_rows)
+        top = tops[c]
+        for d in range(1, BACK + 1):
+            keys = jnp.concatenate([kv[d, 0:HD, :], feat[d]], axis=0)
+            part = jnp.dot(qx[rows, :], keys, preferred_element_type=F32) * factor
+            scores[c, d] = part
+            top = jnp.maximum(top, jnp.maximum(part[:, 0:HD], part[:, HD:]))
+        tops[c] = top
 
     def attend(c):
         ones = jnp.ones((ROWS, HD), BF16)
@@ -239,14 +253,11 @@
             block = jnp.concatenate([kv[d, HD : 2 * HD, 0:HD], kv[d, HD : 2 * HD, HD : 2 * HD]], axis=0)
             vals.append(jnp.concatenate([block, ones], axis=1))
         vals = jnp.concatenate(vals, axis=0)
-        part = []
-        for h in range(PER_CHUNK):
-            rows = slice(h * ROWS, (h + 1) * ROWS)
-            top = jnp.max(tops[c, rows, :], axis=1, keepdims=True)
-            weights = [jnp.exp2(scores[c, d, rows, :] - top).astype(BF16) for d in range(BACK + 1)]
-            mixed = jnp.dot(jnp.concatenate(weights, axis=1), vals, preferred_element_type=F32)
-            part.append((mixed[:, 0:HD] / mixed[:, HD : 2 * HD]).astype(BF16))
-        part = jnp.concatenate(part, axis=1)
+        top = jnp.max(tops[c], axis=1, keepdims=True)
+        weights = [jnp.exp2(scores[c, d] - top).astype(BF16) for d in range(BACK + 1)]
+        mixed = jnp.dot(jnp.concatenate(weights, axis=1), vals, preferred_element_type=F32)
+        mixed = (mixed[:, 0:HD] / mixed[:, HD : 2 * HD]).astype(BF16)
+        part = jnp.concatenate([mixed[h * ROWS : (h + 1) * ROWS, :] for h in range(PER_CHUNK)], axis=1)
         rows = jnp.dot(pack_m[...], part, preferred_element_type=F32).astype(BF16)
         packed[c] = rows.reshape(NCTX, SLOTS, WIDTH)
         landed[c, me] = packed[c, me]
@@ -325,10 +336,19 @@
         def _():
             unpack(s - LAG)
 
+        @pl.when((s >= EARLY) & (s < CHUNKS))
+        def _():
+            score_late(s)
+
         @pl.when(s < CHUNKS)
         def _():
             attend(s)
 
+        @pl.when(s == 0)
+        def _():
+            merge_table()
+            acc[...] = jnp.zeros((ROWS, OUT), F32)
+
         @pl.when((s >= LAG + 1) & (s < CHUNKS + LAG + 1))
         def _():
             forward(s - LAG - 1)
@@ -343,7 +363,6 @@
 
         return carry
 
-    acc[...] = jnp.zeros((ROWS, OUT), F32)
     lax.fori_loop(0, CHUNKS + LAG + 1, step, 0)
     add_columns(CHUNKS - 1, (tp, across), acc)
     from_mate(CHUNKS - 1)

time: 57.4 us -> 56.9 us (level)
  no operation moved by 1% of the time
where the time goes in v7:
time: 56.9 us; the launch traced here: 56.8 us
  Pallas kernels  55.8 us (98%)
  local copies, waits for them, and re-layouts  0.97 us (2%)
    pallas_call x1, Pallas kernels, on_device(): pl.pallas_call(kernel, out_shape=pltpu.VMEM((ROWS, OUT), BF16), in_specs=...  55.8 us

profile of v7, /device:TPU:1, one launch (start us, length us, event | category | flops | bytes accessed | tf_op | source)
XLA Modules:
  0.0 56.8 jit_solution(8112649128701509581)
XLA Ops:
  0.0 55.8 %shard_map.82 = bf16[256,2048]{1,0:T(8,128)(2,1)S(1)} custom-call(s32[64,128]{1,0:T(8,128)} %bitcast.2, s32[64,128]{1,0:T(8,128)} %bitcast.3, bf16[256,1024]{1,0:T(8,128)(2,1)} %q_h.1, bf16[256,128]{1,0:T(8,128)(2,1)} %k_h.1, bf16[256,128]{1,0:T(8,128)(2,1)} %v_h.1, f32[2,256,128]{2,1,0:T(8,128)} %constant.4.clone.inner_h, ...), custom_call_target="tpu_custom_call" | custom-call | flops 7000000000 | bytes 19000000 | tf_op jit(solution)/shard_map/pallas_call | solution.py:386
  55.8 1.0 %copy.10 = bf16[256,2048]{1,0:T(8,128)(2,1)} copy(bf16[256,2048]{1,0:T(8,128)(2,1)S(1)} %shard_map.82) | data formatting | bytes 2097152

commit v8 on v7

--- a/solution.py
+++ b/solution.py
@@ -223,9 +223,9 @@
             key_copy(0, d, me).wait_recv()
 
         keys = jnp.concatenate([kv[d, 0:HD, :], feat[d]], axis=0)
-        every = jnp.dot(qx[0 : EARLY * chunk_rows, :], keys, preferred_element_type=F32) * factor
         for c in range(EARLY):
-            part = every[c * chunk_rows : (c + 1) * chunk_rows, :]
+            rows = slice(c * chunk_rows, (c + 1) * chunk_rows)
+            part = jnp.dot(qx[rows, :], keys, preferred_element_type=F32) * factor
             scores[c, d] = part
             tops[c] = jnp.maximum(tops[c], jnp.maximum(part[:, 0:HD], part[:, HD:]))
         return carry
@@ -253,11 +253,14 @@
             block = jnp.concatenate([kv[d, HD : 2 * HD, 0:HD], kv[d, HD : 2 * HD, HD : 2 * HD]], axis=0)
             vals.append(jnp.concatenate([block, ones], axis=1))
         vals = jnp.concatenate(vals, axis=0)
-        top = jnp.max(tops[c], axis=1, keepdims=True)
-        weights = [jnp.exp2(scores[c, d] - top).astype(BF16) for d in range(BACK + 1)]
-        mixed = jnp.dot(jnp.concatenate(weights, axis=1), vals, preferred_element_type=F32)
-        mixed = (mixed[:, 0:HD] / mixed[:, HD : 2 * HD]).astype(BF16)
-        part = jnp.concatenate([mixed[h * ROWS : (h + 1) * ROWS, :] for h in range(PER_CHUNK)], axis=1)
+        part = []
+        for h in range(PER_CHUNK):
+            rows = slice(h * ROWS, (h + 1) * ROWS)
+            top = jnp.max(tops[c, rows, :], axis=1, keepdims=True)
+            weights = [jnp.exp2(scores[c, d, rows, :] - top).astype(BF16) for d in range(BACK + 1)]
+            mixed = jnp.dot(jnp.concatenate(weights, axis=1), vals, preferred_element_type=F32)
+            part.append((mixed[:, 0:HD] / mixed[:, HD : 2 * HD]).astype(BF16))
+        part = jnp.concatenate(part, axis=1)
         rows = jnp.dot(pack_m[...], part, preferred_element_type=F32).astype(BF16)
         packed[c] = rows.reshape(NCTX, SLOTS, WIDTH)
         landed[c, me] = packed[c, me]
@@ -321,7 +324,7 @@
             target[:, cols] = total.astype(target.dtype)
             return carry
 
-        lax.fori_loop(0, OUT // 512, columns, 0, unroll=2)
+        lax.fori_loop(0, OUT // 512, columns, 0, unroll=4)
 
     def from_mate(c):
         share(c, mate, mate_near).wait_recv()
@@ -363,7 +366,9 @@
 
         return carry
 
-    lax.fori_loop(0, CHUNKS + LAG + 1, step, 0)
+    lax.fori_loop(0, CHUNKS + LAG, step, 0)
+    project(CHUNKS - 2)
+    forward(CHUNKS - 1)
     add_columns(CHUNKS - 1, (tp, across), acc)
     from_mate(CHUNKS - 1)
     add_columns(CHUNKS - 1, (mate, across_mate), out)

time: 56.9 us -> 56 us (0.984)
  Pallas kernels: 55.8 us -> 54.9 us
    pallas_call x1, Pallas kernels: 55.8 us -> 54.9 us  [on_device(): pl.pallas_call(kernel, out_shape=pltpu.VMEM((ROWS, OUT), BF16), in_specs=...]
where the time goes in v8:
time: 56 us; the launch traced here: 55.9 us
  Pallas kernels  54.9 us (98%)
  local copies, waits for them, and re-layouts  0.97 us (2%)
    pallas_call x1, Pallas kernels, on_device(): pl.pallas_call(kernel, out_shape=pltpu.VMEM((ROWS, OUT), BF16), in_specs=...  54.9 us

profile of v8, /device:TPU:1, one launch (start us, length us, event | category | flops | bytes accessed | tf_op | source)
XLA Modules:
  0.0 55.9 jit_solution(18211093799279511528)
XLA Ops:
  0.0 54.9 %shard_map.82 = bf16[256,2048]{1,0:T(8,128)(2,1)S(1)} custom-call(s32[64,128]{1,0:T(8,128)} %bitcast.2, s32[64,128]{1,0:T(8,128)} %bitcast.3, bf16[256,1024]{1,0:T(8,128)(2,1)} %q_h.1, bf16[256,128]{1,0:T(8,128)(2,1)} %k_h.1, bf16[256,128]{1,0:T(8,128)(2,1)} %v_h.1, f32[2,256,128]{2,1,0:T(8,128)} %constant.4.clone.inner_h, ...), custom_call_target="tpu_custom_call" | custom-call | flops 7000000000 | bytes 19000000 | tf_op jit(solution)/shard_map/pallas_call | solution.py:391
  54.9 1.0 %copy.10 = bf16[256,2048]{1,0:T(8,128)(2,1)} copy(bf16[256,2048]{1,0:T(8,128)(2,1)S(1)} %shard_map.82) | data formatting | bytes 2097152

commit v9 on v8

--- a/solution.py
+++ b/solution.py
@@ -52,8 +52,8 @@
 def kernel(
     bl_h, docs_h, q_h, k_h, v_h, inner_h, outer_h, w_hbm, out,
     bl, docs, q_in, k_in, v_in, inner, outer,
-    qx, kv, feat, scores, tops, code, local, pack_m, unpack_m, packed, landed, merged, gath, w, acc,
-    kv_send, kv_recv, a_send, a_recv, n_send, n_recv, z_send, z_recv, c_send, c_recv, f_send, f_recv, w_sem, in_sem, ready,
+    qx, kv, feat, scores, tops, code, local, pack_m, unpack_m, packed, landed, gath, w, acc,
+    kv_send, kv_recv, a_send, a_recv, z_send, z_recv, c_send, c_recv, f_send, f_recv, w_sem, in_sem, ready,
 ):
     me = lax.axis_index("ctx")
     tp = lax.axis_index("tp")
@@ -61,7 +61,6 @@
     mate = hi * 2 + 1 - core
     across = (1 - hi) * 2 + core
     across_mate = (1 - hi) * 2 + 1 - core
-    twin = me + 4 - 8 * ((me // 4) % 2)
 
     w_copy = pltpu.make_async_copy(w_hbm, w, w_sem)
     pairs = (
@@ -85,7 +84,7 @@
         pl.semaphore_signal(barrier, inc=1, device_id=(to, tp), device_id_type=MESH)
         return carry
 
-    for who in ((above, tp), (below, tp), (me, mate), (twin, across)):
+    for who in ((above, tp), (below, tp), (me, mate), (me, across)):
         pl.semaphore_signal(barrier, inc=1, device_id=who, device_id_type=MESH)
     lax.fori_loop(1, BACK, greet, 0)
 
@@ -155,9 +154,13 @@
         qx[rows, HD : 2 * HD] = far
         return carry
 
+    def pass_on():
+        key_copy(0, BACK, me).wait_recv()
+        lax.fori_loop(1, BACK, send_previous, 0)
+
+    pl.when(me >= BACK)(pass_on)
     lax.fori_loop(0, HEADS, queries, 0)
-    key_copy(0, BACK, me).wait_recv()
-    lax.fori_loop(1, BACK, send_previous, 0)
+    pl.when(me < BACK)(pass_on)
 
     doc_iota = iota((HD, ROWS), 0)
 
@@ -182,14 +185,14 @@
     def pack_rows(o, carry):
         hit = code[pl.ds(o, 1), :] == slot_iota
         token = jnp.sum(jnp.where(hit, local[pl.ds(o, 1), :], 0.0), axis=1, keepdims=True)
-        at = pl.multiple_of((o + 4 - 8 * ((o // 4) % 2)) * SLOTS, SLOTS)
+        at = pl.multiple_of(o * SLOTS, SLOTS)
         pack_m[pl.ds(at, SLOTS), :] = jnp.where(token == lane_next, 1.0, 0.0).astype(BF16)
         return carry
 
     lax.fori_loop(0, NCTX, pack_rows, 0, unroll=8)
 
     def merge_table():
-        own = jnp.concatenate([bl[pl.ds(2 * twin, 1), :], bl[pl.ds(2 * twin + 1, 1), :]], axis=1)
+        own = jnp.concatenate([bl[pl.ds(2 * me, 1), :], bl[pl.ds(2 * me + 1, 1), :]], axis=1)
         source_row = (own >> 8).astype(F32)
         source_col = jnp.sum(jnp.where(square_r == square_c, source_row, 0.0), axis=1, keepdims=True)
         earlier = (source_row == source_col) & (square_c < square_r)
@@ -278,41 +281,29 @@
 
         others(send)
 
-    def hand(c, to, sems):
-        return pltpu.make_async_remote_copy(
-            src_ref=merged.at[c],
-            dst_ref=gath.at[c, tp],
-            send_sem=sems[0].at[c],
-            recv_sem=sems[1].at[c],
-            device_id=(twin, to),
-            device_id_type=MESH,
-        )
-
-    near, far_off, mate_near, mate_far = (n_send, n_recv), (z_send, z_recv), (c_send, c_recv), (f_send, f_recv)
-
-    def share(c, slot, sems):
+    def give(c, slot, to, sems):
         return pltpu.make_async_remote_copy(
             src_ref=gath.at[c, slot],
             dst_ref=gath.at[c, slot],
             send_sem=sems[0].at[c],
             recv_sem=sems[1].at[c],
-            device_id=(me, mate),
+            device_id=(me, to),
             device_id_type=MESH,
         )
+
+    far_off, mate_near, mate_far = (z_send, z_recv), (c_send, c_recv), (f_send, f_recv)
 
     def unpack(c):
         rest = packed.at[c, pl.ds(0, NCTX - 1)]
         pltpu.make_async_copy(rest, rest, a_recv.at[c]).wait()
         rows = jnp.dot(unpack_m[...], landed[c].reshape(NCTX * SLOTS, WIDTH), preferred_element_type=F32)
-        merged[c] = rows.astype(BF16)
-        hand(c, tp, near).start()
-        hand(c, across, far_off).start()
+        gath[c, tp] = rows.astype(BF16)
+        give(c, tp, across, far_off).start()
+        give(c, tp, mate, mate_near).start()
 
     def forward(c):
-        hand(c, tp, near).wait_recv()
-        share(c, tp, mate_near).start()
-        hand(c, across, far_off).wait_recv()
-        share(c, across, mate_far).start()
+        give(c, across, across, far_off).wait_recv()
+        give(c, across, mate, mate_far).start()
 
     def add_columns(c, slots, target):
         rows = jnp.concatenate([gath[c, t] for t in slots], axis=1)
@@ -327,8 +318,8 @@
         lax.fori_loop(0, OUT // 512, columns, 0, unroll=4)
 
     def from_mate(c):
-        share(c, mate, mate_near).wait_recv()
-        share(c, across_mate, mate_far).wait_recv()
+        give(c, mate, mate, mate_near).wait_recv()
+        give(c, across_mate, mate, mate_far).wait_recv()
 
     def project(c):
         from_mate(c)
@@ -378,10 +369,9 @@
     for c in range(CHUNKS):
         rest = packed.at[c, pl.ds(0, NCTX - 1)]
         pltpu.make_async_copy(rest, rest, a_send.at[c]).wait()
-        hand(c, tp, near).wait_send()
-        hand(c, across, far_off).wait_send()
-        share(c, tp, mate_near).wait_send()
-        share(c, across, mate_far).wait_send()
+        give(c, tp, across, far_off).wait_send()
+        give(c, tp, mate, mate_near).wait_send()
+        give(c, across, mate, mate_far).wait_send()
 
 
 def on_device(balance_list, doc_ids, raw_queries, raw_keys, values, out_weight):
@@ -412,12 +402,10 @@
             pltpu.VMEM((ROWS, NCTX * SLOTS), BF16),
             pltpu.VMEM((CHUNKS, NCTX, SLOTS, WIDTH), BF16),
             pltpu.VMEM((CHUNKS, NCTX, SLOTS, WIDTH), BF16),
-            pltpu.VMEM((CHUNKS, ROWS, WIDTH), BF16),
             pltpu.VMEM((CHUNKS, 4, ROWS, WIDTH), BF16),
             pltpu.VMEM((4096, OUT), BF16),
             pltpu.VMEM((ROWS, OUT), F32),
             dma((BACK,)), dma((BACK,)),
-            dma((CHUNKS,)), dma((CHUNKS,)),
             dma((CHUNKS,)), dma((CHUNKS,)),
             dma((CHUNKS,)), dma((CHUNKS,)),
             dma((CHUNKS,)), dma((CHUNKS,)),

time: 56 us -> 55.8 us (level)
  no operation moved by 1% of the time
where the time goes in v9:
time: 55.8 us; the launch traced here: 55.6 us
  Pallas kernels  54.7 us (98%)
  local copies, waits for them, and re-layouts  0.97 us (2%)
    pallas_call x1, Pallas kernels, on_device(): pl.pallas_call(kernel, out_shape=pltpu.VMEM((ROWS, OUT), BF16), in_specs=...  54.7 us

profile of v9, /device:TPU:1, one launch (start us, length us, event | category | flops | bytes accessed | tf_op | source)
XLA Modules:
  0.0 55.6 jit_solution(7147339592860268743)
XLA Ops:
  0.0 54.7 %shard_map.82 = bf16[256,2048]{1,0:T(8,128)(2,1)S(1)} custom-call(s32[64,128]{1,0:T(8,128)} %bitcast.2, s32[64,128]{1,0:T(8,128)} %bitcast.3, bf16[256,1024]{1,0:T(8,128)(2,1)} %q_h.1, bf16[256,128]{1,0:T(8,128)(2,1)} %k_h.1, bf16[256,128]{1,0:T(8,128)(2,1)} %v_h.1, f32[2,256,128]{2,1,0:T(8,128)} %constant.4.clone.inner_h, ...), custom_call_target="tpu_custom_call" | custom-call | flops 7000000000 | bytes 19000000 | tf_op jit(solution)/shard_map/pallas_call | solution.py:381
  54.7 1.0 %copy.10 = bf16[256,2048]{1,0:T(8,128)(2,1)} copy(bf16[256,2048]{1,0:T(8,128)(2,1)S(1)} %shard_map.82) | data formatting | bytes 2097152

commit v10 on v9

--- a/solution.py
+++ b/solution.py
@@ -32,7 +32,7 @@
     return min(d % 4, 4 - d % 4) + min(d // 8, 4 - d // 8) + d // 4 % 2
 
 
-FAR_FIRST = sorted(range(1, NCTX), key=hops, reverse=True)
+FAR_FIRST = sorted(range(1, NCTX), key=lambda d: (d // 4 % 2, hops(d)), reverse=True)
 
 
 def rope_tables():
@@ -121,8 +121,21 @@
             device_id_type=MESH,
         )
 
-    key_copy(0, BACK, above).start()
+    first_slab, last_slab = me < BACK, me >= NCTX - BACK
+
+    @pl.when(jnp.logical_not(last_slab))
+    def _():
+        key_copy(0, BACK, above).start()
+
     tell(0)
+
+    def clear(d, carry):
+        @pl.when(first_slab & (d > place_in))
+        def _():
+            kv[d] = jnp.zeros((ROWS, 2 * HD), BF16)
+
+        return carry
+
 
     def send_own(d, carry):
         @pl.when(place_in + d < BACK)
@@ -158,9 +171,9 @@
         key_copy(0, BACK, me).wait_recv()
         lax.fori_loop(1, BACK, send_previous, 0)
 
-    pl.when(me >= BACK)(pass_on)
+    pl.when(jnp.logical_not(first_slab))(pass_on)
+    lax.fori_loop(1, BACK + 1, clear, 0)
     lax.fori_loop(0, HEADS, queries, 0)
-    pl.when(me < BACK)(pass_on)
 
     doc_iota = iota((HD, ROWS), 0)
 
@@ -221,7 +234,7 @@
         part = pl.ds(pl.multiple_of(i * (4096 // BACK), 4096 // BACK), 4096 // BACK)
         pltpu.make_async_copy(w_hbm.at[part, :], w.at[part, :], w_sem).start()
 
-        @pl.when(i > 0)
+        @pl.when((i > 0) & (jnp.logical_not(first_slab) | (d <= place_in)))
         def _():
             key_copy(0, d, me).wait_recv()
 
@@ -364,8 +377,19 @@
     from_mate(CHUNKS - 1)
     add_columns(CHUNKS - 1, (mate, across_mate), out)
 
-    for d in range(1, BACK + 1):
-        key_copy(0, d, me).wait_send()
+    def sent(d, carry):
+        @pl.when((place_in + d < BACK) | jnp.logical_not(first_slab))
+        def _():
+            key_copy(0, d, me).wait_send()
+
+        return carry
+
+    lax.fori_loop(1, BACK, sent, 0)
+
+    @pl.when(jnp.logical_not(last_slab))
+    def _():
+        key_copy(0, BACK, me).wait_send()
+
     for c in range(CHUNKS):
         rest = packed.at[c, pl.ds(0, NCTX - 1)]
         pltpu.make_async_copy(rest, rest, a_send.at[c]).wait()

time: 55.8 us -> 55 us (0.986)
  Pallas kernels: 54.7 us -> 53.9 us
    pallas_call x1, Pallas kernels: 54.7 us -> 53.9 us  [on_device(): pl.pallas_call(kernel, out_shape=pltpu.VMEM((ROWS, OUT), BF16), in_specs=...]
where the time goes in v10:
time: 55 us; the launch traced here: 54.9 us
  Pallas kernels  53.9 us (98%)
  local copies, waits for them, and re-layouts  0.97 us (2%)
    pallas_call x1, Pallas kernels, on_device(): pl.pallas_call(kernel, out_shape=pltpu.VMEM((ROWS, OUT), BF16), in_specs=...  53.9 us

profile of v10, /device:TPU:1, one launch (start us, length us, event | category | flops | bytes accessed | tf_op | source)
XLA Modules:
  0.0 54.9 jit_solution(7306007138448662243)
XLA Ops:
  0.0 53.9 %shard_map.82 = bf16[256,2048]{1,0:T(8,128)(2,1)S(1)} custom-call(s32[64,128]{1,0:T(8,128)} %bitcast.2, s32[64,128]{1,0:T(8,128)} %bitcast.3, bf16[256,1024]{1,0:T(8,128)(2,1)} %q_h.1, bf16[256,128]{1,0:T(8,128)(2,1)} %k_h.1, bf16[256,128]{1,0:T(8,128)(2,1)} %v_h.1, f32[2,256,128]{2,1,0:T(8,128)} %constant.4.clone.inner_h, ...), custom_call_target="tpu_custom_call" | custom-call | flops 7000000000 | bytes 19000000 | tf_op jit(solution)/shard_map/pallas_call | solution.py:405
  53.9 1.0 %copy.10 = bf16[256,2048]{1,0:T(8,128)(2,1)} copy(bf16[256,2048]{1,0:T(8,128)(2,1)S(1)} %shard_map.82) | data formatting | bytes 2097152

commit v11 on v10

--- a/solution.py
+++ b/solution.py
@@ -18,7 +18,7 @@
 SLOTS = 16
 CHUNKS = 4
 LAG = 3
-EARLY = 2
+EARLY = 3
 PER_CHUNK = HEADS // CHUNKS
 WIDTH = HEADS * HD // CHUNKS
 OUT = 2048
@@ -332,10 +332,13 @@
 
     def from_mate(c):
         give(c, mate, mate, mate_near).wait_recv()
+
+    def from_far(c):
         give(c, across_mate, mate, mate_far).wait_recv()
 
     def project(c):
         from_mate(c)
+        from_far(c)
         add_columns(c, range(4), acc)
 
     def step(s, carry):
@@ -372,10 +375,12 @@
 
     lax.fori_loop(0, CHUNKS + LAG, step, 0)
     project(CHUNKS - 2)
+    from_mate(CHUNKS - 1)
+    add_columns(CHUNKS - 1, (tp, mate), acc)
     forward(CHUNKS - 1)
-    add_columns(CHUNKS - 1, (tp, across), acc)
-    from_mate(CHUNKS - 1)
-    add_columns(CHUNKS - 1, (mate, across_mate), out)
+    add_columns(CHUNKS - 1, (across,), acc)
+    from_far(CHUNKS - 1)
+    add_columns(CHUNKS - 1, (across_mate,), out)
 
     def sent(d, carry):
         @pl.when((place_in + d < BACK) | jnp.logical_not(first_slab))

time: 55 us -> 55.9 us (1.016)
  Pallas kernels: 53.9 us -> 54.8 us
    pallas_call x1, Pallas kernels: 53.9 us -> 54.8 us  [on_device(): pl.pallas_call(kernel, out_shape=pltpu.VMEM((ROWS, OUT), BF16), in_specs=...]
where the time goes in v11:
time: 55.9 us; the launch traced here: 55.8 us
  Pallas kernels  54.8 us (98%)
  local copies, waits for them, and re-layouts  0.97 us (2%)
    pallas_call x1, Pallas kernels, on_device(): pl.pallas_call(kernel, out_shape=pltpu.VMEM((ROWS, OUT), BF16), in_specs=...  54.8 us

profile of v11, /device:TPU:1, one launch (start us, length us, event | category | flops | bytes accessed | tf_op | source)
XLA Modules:
  0.0 55.8 jit_solution(7667373213172430236)
XLA Ops:
  0.0 54.8 %shard_map.82 = bf16[256,2048]{1,0:T(8,128)(2,1)S(1)} custom-call(s32[64,128]{1,0:T(8,128)} %bitcast.2, s32[64,128]{1,0:T(8,128)} %bitcast.3, bf16[256,1024]{1,0:T(8,128)(2,1)} %q_h.1, bf16[256,128]{1,0:T(8,128)(2,1)} %k_h.1, bf16[256,128]{1,0:T(8,128)(2,1)} %v_h.1, f32[2,256,128]{2,1,0:T(8,128)} %constant.4.clone.inner_h, ...), custom_call_target="tpu_custom_call" | custom-call | flops 7000000000 | bytes 19000000 | tf_op jit(solution)/shard_map/pallas_call | solution.py:410
  54.9 1.0 %copy.10 = bf16[256,2048]{1,0:T(8,128)(2,1)} copy(bf16[256,2048]{1,0:T(8,128)(2,1)S(1)} %shard_map.82) | data formatting | bytes 2097152

commit v12 on v10

--- a/solution.py
+++ b/solution.py
@@ -18,7 +18,7 @@
 SLOTS = 16
 CHUNKS = 4
 LAG = 3
-EARLY = 2
+EARLY = 1
 PER_CHUNK = HEADS // CHUNKS
 WIDTH = HEADS * HD // CHUNKS
 OUT = 2048

time: 55 us -> 55.3 us (level)
  no operation moved by 1% of the time
where the time goes in v12:
time: 55.3 us; the launch traced here: 55.2 us
  Pallas kernels  54.2 us (98%)
  local copies, waits for them, and re-layouts  0.97 us (2%)
    pallas_call x1, Pallas kernels, on_device(): pl.pallas_call(kernel, out_shape=pltpu.VMEM((ROWS, OUT), BF16), in_specs=...  54.2 us

profile of v12, /device:TPU:1, one launch (start us, length us, event | category | flops | bytes accessed | tf_op | source)
XLA Modules:
  0.0 55.2 jit_solution(6750301551321044652)
XLA Ops:
  0.0 54.2 %shard_map.82 = bf16[256,2048]{1,0:T(8,128)(2,1)S(1)} custom-call(s32[64,128]{1,0:T(8,128)} %bitcast.2, s32[64,128]{1,0:T(8,128)} %bitcast.3, bf16[256,1024]{1,0:T(8,128)(2,1)} %q_h.1, bf16[256,128]{1,0:T(8,128)(2,1)} %k_h.1, bf16[256,128]{1,0:T(8,128)(2,1)} %v_h.1, f32[2,256,128]{2,1,0:T(8,128)} %constant.4.clone.inner_h, ...), custom_call_target="tpu_custom_call" | custom-call | flops 7000000000 | bytes 19000000 | tf_op jit(solution)/shard_map/pallas_call | solution.py:405
  54.2 1.0 %copy.10 = bf16[256,2048]{1,0:T(8,128)(2,1)} copy(bf16[256,2048]{1,0:T(8,128)(2,1)S(1)} %shard_map.82) | data formatting | bytes 2097152
